TPU v7x, 32 devices: a whole 2x2x4 slice. The times are simulated.
32 devices in a mesh: ctx: 8 (over z, y), head: 4 (over x, core).
Axes of the slice: x: 2, y: 2, z: 4, core: 2. Of those that a mesh axis runs over, the one named last changes fastest.
Arguments:
- queries: bfloat16 [2048, 32, 128], P('ctx', 'head'), may hold values from -6 to 6
- key_states: bfloat16 [2048, 4, 128], P('ctx', 'head'), may hold values from -6 to 6
- value_states: bfloat16 [2048, 4, 128], P('ctx', 'head'), may hold values from -6 to 6
- doc_lengths: int32 [8], replicated, may hold values from 1 to 1792, 2048 in all
- grad_attended: bfloat16 [2048, 4096], P(('ctx', 'head')), may hold values from -6 to 6
Outputs:
- attended: bfloat16 [2048, 4096], P(('ctx', 'head'))
- grad_queries: bfloat16 [2048, 32, 128], P('ctx', 'head')
- grad_keys: bfloat16 [2048, 4, 128], P('ctx', 'head')
- grad_values: bfloat16 [2048, 4, 128], P('ctx', 'head')
All inputs are finite; a program needn't handle non-finite values.
Results may differ from a plain program's by a relative error of at most 0.022.
Values may be sent and summed in bfloat16 or wider, within the bound.
No kernel may reach another device: no remote copies, remote signals or barrier semaphores. Data moves between devices by JAX's collectives and lax.ppermute only.
A program may use at most 64 MiB of HBM per device.

v0:
```python
import functools
import math

import jax
import jax.numpy as jnp
from jax import lax
from jax.experimental import pallas as pl
from jax.experimental.pallas import tpu as pltpu
from jax.sharding import PartitionSpec as P

DOC_MOST = 1792
NEG_FILL = -1e30
TILE = 256
ONES = 16
LOG2_E = 1.4426950408889634


def dot(a, b):
    return jnp.dot(a, b, preferred_element_type=jnp.float32)


def dot_nt(a, b):
    return lax.dot_general(a, b, (((1,), (1,)), ((), ())), preferred_element_type=jnp.float32)


def unit(size):
    rows = lax.broadcasted_iota(jnp.int32, (size, size), 0)
    return (rows == lax.broadcasted_iota(jnp.int32, (size, size), 1)).astype(jnp.bfloat16)


def less(tile, row8):
    rows, columns = tile.shape
    return (tile.reshape(rows // 8, 8, columns) - row8[None]).reshape(rows, columns)


def attention_kernel(
    doc_ref,
    place_ref,
    q_ref,
    do_ref,
    own_ref,
    near_ref,
    far_ref,
    *refs,
    back,
    heads,
    width,
    scale,
):
    arrived = refs[:back]
    (o_ref, dq_ref, dmine_ref, dother_ref) = refs[back : back + 4]
    (
        q32,
        keys,
        values,
        kt,
        vt,
        q_rows,
        do_rows,
        q_cols,
        do_cols,
        scores,
        probs,
        d_scores,
        accum,
        top,
        delta,
    ) = refs[back + 4 :]
    tok = q_ref.shape[0]
    docs = doc_ref.shape[0]
    base = place_ref[0]
    own = place_ref[1]
    parity = place_ref[2]
    small, large = unit(width), unit(tok)

    for pair in range(back + 1):
        k = back - pair
        mine = own_ref[...] if k == 0 else arrived[k - 1][...]
        other = near_ref[...] if k == 0 else far_ref[2 * tok * (k - 1) : 2 * tok * k, :]
        for block, place in ((mine, 2 * pair + parity), (other, 2 * pair + 1 - parity)):
            at = pl.ds(pl.multiple_of(place * tok, tok), tok)
            keys[at, :] = block[:tok]
            values[at, :] = block[tok:]

    q32[...] = q_ref[...].astype(jnp.float32)
    accum[...] = jnp.zeros_like(accum)
    top[...] = jnp.full_like(top, NEG_FILL)
    for j in range(heads):
        part = pl.ds(j * tok, tok)
        q_part = q32[:, j, :].astype(jnp.bfloat16)
        do_part = do_ref[:, j * width : (j + 1) * width]
        q_rows[part, :] = q_part
        do_rows[part, :] = do_part
        q_cols[:, part] = dot_nt(small, q_part).astype(jnp.bfloat16)
        do_cols[:, part] = dot_nt(small, do_part).astype(jnp.bfloat16)

    t_first = base + own * TILE
    t_row = t_first + lax.broadcasted_iota(jnp.int32, (1, tok), 1)
    end = jnp.int32(0)
    start_first, start_last = jnp.int32(0), jnp.int32(0)
    start_row = jnp.zeros((1, tok), jnp.int32)
    for i in range(docs):
        end = end + doc_ref[i]
        start_first = jnp.where(end <= t_first, end, start_first)
        start_last = jnp.where(end <= t_first + tok - 1, end, start_last)
        start_row = jnp.where(t_row >= end, end, start_row)
    low = jnp.maximum(start_first - base, 0) // TILE
    clear = jnp.clip((start_last - base + TILE - 1) // TILE, low, own)

    def score_tile(i, masked):
        at = pl.ds(pl.multiple_of(i * TILE, TILE), TILE)
        key_tile, value_tile = keys[at, :], values[at, :]
        kt[:, at] = dot_nt(small, key_tile).astype(jnp.bfloat16)
        vt[0:width, at] = dot_nt(small, value_tile).astype(jnp.bfloat16)
        vt[width:, at] = jnp.ones((ONES, TILE), jnp.bfloat16)
        if masked:
            s_col = base + i * TILE + lax.broadcasted_iota(jnp.int32, (TILE, tok), 0)
            live = (s_col >= start_row) & (s_col <= t_row)
        for j in range(heads):
            part = pl.ds(j * tok, tok)
            tile = dot(key_tile, q_cols[:, part]) * (scale * LOG2_E)
            if masked:
                tile = jnp.where(live, tile, NEG_FILL)
            scores[at, part] = tile
            top[:, part] = jnp.maximum(
                top[:, part], jnp.max(tile.reshape(TILE // 8, 8, tok), axis=0)
            )

    def edge_step(n, carry):
        score_tile(jnp.where(n < clear - low, low + n, own), True)
        return carry

    def inner_step(i, carry):
        score_tile(i, False)
        return carry

    lax.fori_loop(0, clear - low + 1, edge_step, 0)
    lax.fori_loop(clear, own, inner_step, 0)
    top[...] = jnp.broadcast_to(jnp.max(top[...], axis=0, keepdims=True), top.shape)

    def weigh_step(i, carry):
        at = pl.ds(pl.multiple_of(i * TILE, TILE), TILE)
        for j in range(heads):
            part = pl.ds(j * tok, tok)
            weights = jnp.exp2(less(scores[at, part], top[:, part])).astype(jnp.bfloat16)
            accum[:, part] += dot(vt[:, at], weights)
        return carry

    lax.fori_loop(low, own + 1, weigh_step, 0)

    for j in range(heads):
        part = pl.ds(j * tok, tok)
        total = accum[width : width + 8, part]
        out = (accum[0:width, part] * (1.0 / total[0:1])).astype(jnp.bfloat16)
        o_ref[:, j * width : (j + 1) * width] = dot_nt(large, out).astype(jnp.bfloat16)
        product = do_cols[:, part].astype(jnp.float32) * out.astype(jnp.float32)
        delta[:, part] = jnp.broadcast_to(jnp.sum(product, axis=0, keepdims=True), (8, tok))
        top[:, part] = top[:, part] + jnp.log2(total)
    accum[...] = jnp.zeros_like(accum)

    def put(i, d_keys, d_values):
        to = pl.ds(pl.multiple_of((i // 2) * tok, tok), tok)

        @pl.when(i % 2 == parity)
        def _():
            dmine_ref[to, 0:width] = d_keys
            dmine_ref[to, width:] = d_values

        @pl.when(i % 2 != parity)
        def _():
            dother_ref[to, 0:width] = d_keys.astype(jnp.bfloat16)
            dother_ref[to, width:] = d_values.astype(jnp.bfloat16)

    def empty_step(i, carry):
        zero = jnp.zeros((tok, width), jnp.float32)
        put(i, zero, zero)
        return carry

    def back_step(i, carry):
        at = pl.ds(pl.multiple_of(i * TILE, TILE), TILE)
        value_tile = values[at, :]
        for j in range(heads):
            part = pl.ds(j * tok, tok)
            tile = jnp.exp2(less(scores[at, part], top[:, part]))
            d_probs = dot(value_tile, do_cols[:, part])
            d_tile = (tile * less(d_probs, delta[:, part])).astype(jnp.bfloat16)
            probs[:, part] = tile.astype(jnp.bfloat16)
            d_scores[:, part] = d_tile
            accum[0:width, part] += dot(kt[:, at], d_tile)
        put(i, dot(d_scores[...], q_rows[...]) * scale, dot(probs[...], do_rows[...]))
        return carry

    lax.fori_loop(0, low, empty_step, 0)
    lax.fori_loop(own + 1, 2 * back + 2, empty_step, 0)
    lax.fori_loop(low, own + 1, back_step, 0)
    for j in range(heads):
        d_part = (accum[0:width, j * tok : (j + 1) * tok] * scale).astype(jnp.bfloat16)
        q32[:, j, :] = dot_nt(large, d_part)
    dq_ref[...] = q32[...].astype(jnp.bfloat16)


def attend(doc_lengths, place, queries, grad_rows, own, near, far, arrived):
    tok, heads, width = queries.shape
    back = len(arrived)
    half = (back + 1) * tok
    span = 2 * half
    rows = heads * tok
    vmem = pl.BlockSpec(memory_space=pltpu.VMEM)
    smem = pl.BlockSpec(memory_space=pltpu.SMEM)
    return pl.pallas_call(
        functools.partial(
            attention_kernel,
            back=back,
            heads=heads,
            width=width,
            scale=1.0 / math.sqrt(width),
        ),
        out_shape=(
            jax.ShapeDtypeStruct((tok, heads * width), jnp.bfloat16),
            jax.ShapeDtypeStruct((tok, heads, width), jnp.bfloat16),
            jax.ShapeDtypeStruct((half, 2 * width), jnp.float32),
            jax.ShapeDtypeStruct((half, 2 * width), jnp.bfloat16),
        ),
        in_specs=[smem, smem] + [vmem] * (5 + back),
        out_specs=(vmem, vmem, vmem, vmem),
        scratch_shapes=[
            pltpu.VMEM((tok, heads, width), jnp.float32),
            pltpu.VMEM((span, width), jnp.bfloat16),
            pltpu.VMEM((span, width), jnp.bfloat16),
            pltpu.VMEM((width, span), jnp.bfloat16),
            pltpu.VMEM((width + ONES, span), jnp.bfloat16),
            pltpu.VMEM((rows, width), jnp.bfloat16),
            pltpu.VMEM((rows, width), jnp.bfloat16),
            pltpu.VMEM((width, rows), jnp.bfloat16),
            pltpu.VMEM((width, rows), jnp.bfloat16),
            pltpu.VMEM((span, rows), jnp.float32),
            pltpu.VMEM((TILE, rows), jnp.bfloat16),
            pltpu.VMEM((TILE, rows), jnp.bfloat16),
            pltpu.VMEM((width + ONES, rows), jnp.float32),
            pltpu.VMEM((8, rows), jnp.float32),
            pltpu.VMEM((8, rows), jnp.float32),
        ],
        compiler_params=pltpu.CompilerParams(vmem_limit_bytes=50 * 1024 * 1024),
        cost_estimate=pl.CostEstimate(
            flops=14 * tok * heads * width * span,
            bytes_accessed=4 * tok * heads * width * 2 + 4 * span * width * 2,
            transcendentals=tok * heads * span,
        ),
        name="attention",
    )(doc_lengths, place, queries, grad_rows, own, near, far, *arrived)


def shifted(block, by, count):
    pairs = [(i, i + by) for i in range(count) if 0 <= i + by < count]
    return lax.ppermute(block, "ctx", pairs)


def exchanged(block, count):
    return lax.ppermute(block, "ctx", [(i, i ^ 1) for i in range(count)])


def body(queries, key_states, value_states, doc_lengths, grad_attended):
    tok, heads, width = queries.shape
    count = lax.axis_size("ctx")
    ctx = lax.axis_index("ctx")
    reach = min((DOC_MOST + tok - 2) // tok, count - 1)
    back = min((reach + 1) // 2, count // 2 - 1)
    own = jnp.concatenate(
        [key_states.reshape(tok, width), value_states.reshape(tok, width)], axis=0
    )
    near = exchanged(own, count)
    arrived = [shifted(own, 2 * k, count) for k in range(1, back + 1)]
    near, arrived, grad_attended = lax.optimization_barrier((near, arrived, grad_attended))
    far = exchanged(jnp.concatenate(arrived, axis=0), count)
    grad_rows = lax.all_to_all(grad_attended, "head", split_axis=1, concat_axis=0, tiled=True)
    parity = ctx % 2
    place = jnp.stack([(ctx - parity - 2 * back) * tok, 2 * back + parity, parity])
    attended, grad_queries, d_mine, d_other = attend(
        doc_lengths, place.astype(jnp.int32), queries, grad_rows, own, near, far, arrived
    )
    d_near = exchanged(d_other, count)
    attended = lax.all_to_all(attended, "head", split_axis=0, concat_axis=1, tiled=True)
    total = (d_mine + d_near.astype(jnp.float32)).reshape(back + 1, tok, 2 * width)
    own_total = total[back]
    for k in range(back, 0, -1):
        own_total = own_total + shifted(
            total[back - k].astype(jnp.bfloat16), -2 * k, count
        ).astype(jnp.float32)
    own_total = own_total.astype(jnp.bfloat16)
    grad_keys = own_total[:, :width].reshape(tok, 1, width)
    grad_values = own_total[:, width:].reshape(tok, 1, width)
    return attended, grad_queries, grad_keys, grad_values


def solution(mesh):
    in_specs = (
        P("ctx", "head", None),
        P("ctx", "head", None),
        P("ctx", "head", None),
        P(),
        P(("ctx", "head"), None),
    )
    out_specs = (
        P(("ctx", "head"), None),
        P("ctx", "head", None),
        P("ctx", "head", None),
        P("ctx", "head", None),
    )
    return jax.shard_map(body, mesh=mesh, in_specs=in_specs, out_specs=out_specs, check_vma=False)
```

profile of v0, /device:TPU:0, one launch (start us, length us, event | category | flops | bytes accessed | tf_op | source)
XLA Modules:
  0.0 90.0 jit_solution(6096837734497176218)
XLA Ops:
  0.6 0.0 copy-start.3
  0.6 0.9 %pad_maximum_fusion.1.own_ref = bf16[512,128]{1,0:T(8,128)(2,1)S(1)} fusion(bf16[256,128]{1,0:T(8,128)(2,1)} %bitcast.24, bf16[256,128]{1,0:T(8,128)(2,1)} %bitcast.25), kind=kLoop, calls=%fused_computation.7 | loop fusion | flops 262144 | bytes 262144 | tf_op jit(solution)/shard_map/concatenate | solution.py:268
  1.6 7.0 %collective-permute-start.3 = (bf16[512,128]{1,0:T(8,128)(2,1)S(1)}, bf16[512,128]{1,0:T(8,128)(2,1)S(1)}, u32[]{:S(2)}, u32[]{:S(2)}) collective-permute-start(bf16[512,128]{1,0:T(8,128)(2,1)S(1)} %pad_maximum_fusion.1.own_ref), channel_id=1, source_target_pairs={{0,24},{4,28},{1,25},{5,29},{2,26},{6,30},{3,27},{7,31}} | collective-permute-start | bytes 393224 | tf_op jit(solution)/shard_map/ppermute | solution.py:255
  8.6 1.3 %collective-permute-start.2 = (bf16[512,128]{1,0:T(8,128)(2,1)S(1)}, bf16[512,128]{1,0:T(8,128)(2,1)S(1)}, u32[]{:S(2)}, u32[]{:S(2)}) collective-permute-start(bf16[512,128]{1,0:T(8,128)(2,1)S(1)} %pad_maximum_fusion.1.own_ref), channel_id=1, source_target_pairs={{0,16},{4,20},{8,24},{12,28},{1,17},{5,21},{9,25},{13,29},{2,18},{... | collective-permute-start | bytes 393224 | tf_op jit(solution)/shard_map/ppermute | solution.py:255
  9.9 2.5 %collective-permute-start.1 = (bf16[512,128]{1,0:T(8,128)(2,1)S(1)}, bf16[512,128]{1,0:T(8,128)(2,1)S(1)}, u32[]{:S(2)}, u32[]{:S(2)}) collective-permute-start(bf16[512,128]{1,0:T(8,128)(2,1)S(1)} %pad_maximum_fusion.1.own_ref), channel_id=1, source_target_pairs={{0,8},{4,12},{8,16},{12,20},{16,24},{20,28},{1,9},{5,13},{9,17},{1... | collective-permute-start | bytes 393224 | tf_op jit(solution)/shard_map/ppermute | solution.py:255
  12.3 1.6 %collective-permute-start = (bf16[512,128]{1,0:T(8,128)(2,1)S(1)}, bf16[512,128]{1,0:T(8,128)(2,1)S(1)}, u32[]{:S(2)}, u32[]{:S(2)}) collective-permute-start(bf16[512,128]{1,0:T(8,128)(2,1)S(1)} %pad_maximum_fusion.1.own_ref), channel_id=1, source_target_pairs={{0,4},{4,0},{8,12},{12,8},{16,20},{20,16},{24,28},{28,24},{1,5},{5... | collective-permute-start | bytes 393224 | tf_op jit(solution)/shard_map/ppermute | solution.py:259
  13.9 0.0 collective-permute-done.3.refs_2_
  13.9 1.4 %collective-permute-done.2.refs_1_ = bf16[512,128]{1,0:T(8,128)(2,1)S(1)} collective-permute-done((bf16[512,128]{1,0:T(8,128)(2,1)S(1)}, bf16[512,128]{1,0:T(8,128)(2,1)S(1)}, u32[]{:S(2)}, u32[]{:S(2)}) %collective-permute-start.2) | collective-permute-done | bytes 131104 | tf_op jit(solution)/shard_map/ppermute | solution.py:255
  15.3 1.7 %collective-permute-done.1.refs_0_ = bf16[512,128]{1,0:T(8,128)(2,1)S(1)} collective-permute-done((bf16[512,128]{1,0:T(8,128)(2,1)S(1)}, bf16[512,128]{1,0:T(8,128)(2,1)S(1)}, u32[]{:S(2)}, u32[]{:S(2)}) %collective-permute-start.1) | collective-permute-done | bytes 131104 | tf_op jit(solution)/shard_map/ppermute | solution.py:255
  16.9 0.4 collective-permute-done.near_ref
  17.4 1.6 %collective-permute-start.4 = (bf16[1536,128]{1,0:T(8,128)(2,1)S(1)}, bf16[1536,128]{1,0:T(8,128)(2,1)S(1)}, u32[]{:S(2)}, u32[]{:S(2)}) collective-permute-start(bf16[1536,128]{1,0:T(8,128)(2,1)S(1)} %pad_maximum_fusion), channel_id=1, source_target_pairs={{0,4},{4,0},{8,12},{12,8},{16,20},{20,16},{24,28},{28,24},{1,5},{5... | collective-permute-start | bytes 1179656 | tf_op jit(solution)/shard_map/ppermute | solution.py:259
  19.0 0.0 copy-done.3
  19.0 0.8 copy.14
  19.8 0.0 copy-start
  19.8 3.6 %all-to-all-start = ((bf16[64,4,1024]{2,0,1:T(8,128)(2,1)}), bf16[64,4,1024]{2,0,1:T(8,128)(2,1)S(1)}, u32[]{:S(2)}, u32[]{:S(2)}) async-start(bf16[64,4,1024]{2,0,1:T(8,128)(2,1)} %bitcast.19), calls=%async_computation | async-start | bytes 1048576 | tf_op jit(solution)/shard_map/all_to_all | solution.py:275
  23.4 0.1 pad_add_fusion.place_ref
  23.5 0.0 copy-start.1
  23.5 3.5 %collective-permute-done.4.far_ref = bf16[1536,128]{1,0:T(8,128)(2,1)S(1)} collective-permute-done((bf16[1536,128]{1,0:T(8,128)(2,1)S(1)}, bf16[1536,128]{1,0:T(8,128)(2,1)S(1)}, u32[]{:S(2)}, u32[]{:S(2)}) %collective-permute-start.4) | collective-permute-done | bytes 393248 | tf_op jit(solution)/shard_map/ppermute | solution.py:259
  27.0 5.2 %all-to-all-done = bf16[64,4,1024]{2,0,1:T(8,128)(2,1)S(1)} async-done(((bf16[64,4,1024]{2,0,1:T(8,128)(2,1)}), bf16[64,4,1024]{2,0,1:T(8,128)(2,1)S(1)}, u32[]{:S(2)}, u32[]{:S(2)}) %all-to-all-start) | async-done | bytes 524320 | tf_op jit(solution)/shard_map/all_to_all | solution.py:275
  32.2 0.0 copy-done
  32.2 0.0 copy-done.1
  32.2 8.5 %attention.1 = (bf16[256,1024]{1,0:T(8,128)(2,1)}, bf16[256,8,128]{2,1,0:T(8,128)(2,1)}, f32[1024,256]{1,0:T(8,128)}, bf16[1024,256]{1,0:T(8,128)(2,1)S(1)}) custom-call(s32[8]{0:T(128)S(1)} %copy-done.1, s32[3]{0:T(128)S(1)} %pad_add_fusion.place_ref, bf16[256,8,128]{2,1,0:T(8,128)(2,1)S(1)} %copy-done, bf16[256,1024]{1,0:T(8,128)(2,1)S(1)} %bitcast.20, ...), custom_call_target="tpu_custom_call" | custom-call | flops 7516192768 | bytes 4194304 | tf_op jit(solution)/shard_map/attention/pallas_call | solution.py:210
  40.7 0.0 copy-start.2
  40.7 4.0 %collective-permute-start.5 = (bf16[1024,256]{1,0:T(8,128)(2,1)S(1)}, bf16[1024,256]{1,0:T(8,128)(2,1)S(1)}, u32[]{:S(2)}, u32[]{:S(2)}) collective-permute-start(bf16[1024,256]{1,0:T(8,128)(2,1)S(1)} %get-tuple-element.21), channel_id=1, source_target_pairs={{0,4},{4,0},{8,12},{12,8},{16,20},{20,16},{24,28},{28,24},{1,5},{5... | collective-permute-start | bytes 1572872 | tf_op jit(solution)/shard_map/ppermute | solution.py:259
  44.7 3.5 %all-to-all-start.1 = ((bf16[4,64,1024]{2,1,0:T(8,128)(2,1)}), bf16[4,64,1024]{2,1,0:T(8,128)(2,1)S(1)}, u32[]{:S(2)}, u32[]{:S(2)}) async-start(bf16[4,64,1024]{2,1,0:T(8,128)(2,1)} %bitcast.7), calls=%async_computation.1 | async-start | bytes 1048576 | tf_op jit(solution)/shard_map/all_to_all | solution.py:282
  48.2 8.2 %collective-permute-done.5 = bf16[1024,256]{1,0:T(8,128)(2,1)S(1)} collective-permute-done((bf16[1024,256]{1,0:T(8,128)(2,1)S(1)}, bf16[1024,256]{1,0:T(8,128)(2,1)S(1)}, u32[]{:S(2)}, u32[]{:S(2)}) %collective-permute-start.5) | collective-permute-done | bytes 524320 | tf_op jit(solution)/shard_map/ppermute | solution.py:259
  56.4 0.0 copy-start.4
  56.4 0.8 copy-done.4
  57.2 0.0 copy-done.2
  57.2 1.2 %fusion.3 = (bf16[1024,256]{1,0:T(8,128)(2,1)S(1)}, f32[1024,256]{1,0:T(8,128)S(1)}) fusion(f32[1024,256]{1,0:T(8,128)S(1)} %copy-done.2, bf16[1024,256]{1,0:T(8,128)(2,1)} %copy-done.4), kind=kLoop, calls=%fused_computation.11 | loop fusion | flops 786432 | bytes 3145728 | tf_op jit(solution)/shard_map/convert.2
  58.4 1.3 %collective-permute-start.6 = (bf16[256,256]{1,0:T(8,128)(2,1)S(1)}, bf16[256,256]{1,0:T(8,128)(2,1)S(1)}, u32[]{:S(2)}, u32[]{:S(2)}) collective-permute-start(bf16[256,256]{1,0:T(8,128)(2,1)S(1)} %get-tuple-element.24), channel_id=1, source_target_pairs={{24,0},{28,4},{25,1},{29,5},{26,2},{30,6},{27,3},{31,7}} | collective-permute-start | bytes 393224 | tf_op jit(solution)/shard_map/ppermute | solution.py:255
  59.7 1.3 %collective-permute-start.8 = (bf16[256,256]{1,0:T(8,128)(2,1)S(1)}, bf16[256,256]{1,0:T(8,128)(2,1)S(1)}, u32[]{:S(2)}, u32[]{:S(2)}) collective-permute-start(bf16[256,256]{1,0:T(8,128)(2,1)S(1)} %get-tuple-element.25), channel_id=1, source_target_pairs={{8,0},{12,4},{16,8},{20,12},{24,16},{28,20},{9,1},{13,5},{17,9},{2... | collective-permute-start | bytes 393224 | tf_op jit(solution)/shard_map/ppermute | solution.py:255
  61.0 1.3 %collective-permute-start.7 = (bf16[256,256]{1,0:T(8,128)(2,1)S(1)}, bf16[256,256]{1,0:T(8,128)(2,1)S(1)}, u32[]{:S(2)}, u32[]{:S(2)}) collective-permute-start(bf16[256,256]{1,0:T(8,128)(2,1)S(1)} %get-tuple-element.26), channel_id=1, source_target_pairs={{16,0},{20,4},{24,8},{28,12},{17,1},{21,5},{25,9},{29,13},{18,2},{... | collective-permute-start | bytes 393224 | tf_op jit(solution)/shard_map/ppermute | solution.py:255
  62.3 0.0 all-to-all-done.1
  62.3 0.8 copy.12
  63.2 25.5 %collective-permute-done.6 = bf16[256,256]{1,0:T(8,128)(2,1)S(1)} collective-permute-done((bf16[256,256]{1,0:T(8,128)(2,1)S(1)}, bf16[256,256]{1,0:T(8,128)(2,1)S(1)}, u32[]{:S(2)}, u32[]{:S(2)}) %collective-permute-start.6) | collective-permute-done | bytes 131104 | tf_op jit(solution)/shard_map/ppermute | solution.py:255
  88.7 0.0 collective-permute-done.8
  88.7 0.6 collective-permute-done.7
  89.3 0.1 fusion.2
  89.4 0.7 slice_bitcast_fusion
  (2 shorter events, 0.1 us)
Async XLA Ops:
  0.6 18.4 %copy-start.3 = (bf16[64,4096]{1,0:T(8,128)(2,1)S(1)}, bf16[64,4096]{1,0:T(8,128)(2,1)}, u32[]{:S(2)}) copy-start(bf16[64,4096]{1,0:T(8,128)(2,1)} %param.9) | copy-start | bytes 1572868
  1.6 12.3 %collective-permute-start.3 = (bf16[512,128]{1,0:T(8,128)(2,1)S(1)}, bf16[512,128]{1,0:T(8,128)(2,1)S(1)}, u32[]{:S(2)}, u32[]{:S(2)}) collective-permute-start(bf16[512,128]{1,0:T(8,128)(2,1)S(1)} %pad_maximum_fusion.1.own_ref), channel_id=1, source_target_pairs={{0,24},{4,28},{1,25},{5,29},{2,26},{6,30},{3,27},{7,31}} | collective-permute-start | bytes 393224 | tf_op jit(solution)/shard_map/ppermute | solution.py:255
  8.6 6.7 %collective-permute-start.2 = (bf16[512,128]{1,0:T(8,128)(2,1)S(1)}, bf16[512,128]{1,0:T(8,128)(2,1)S(1)}, u32[]{:S(2)}, u32[]{:S(2)}) collective-permute-start(bf16[512,128]{1,0:T(8,128)(2,1)S(1)} %pad_maximum_fusion.1.own_ref), channel_id=1, source_target_pairs={{0,16},{4,20},{8,24},{12,28},{1,17},{5,21},{9,25},{13,29},{2,18},{... | collective-permute-start | bytes 393224 | tf_op jit(solution)/shard_map/ppermute | solution.py:255
  9.9 7.1 %collective-permute-start.1 = (bf16[512,128]{1,0:T(8,128)(2,1)S(1)}, bf16[512,128]{1,0:T(8,128)(2,1)S(1)}, u32[]{:S(2)}, u32[]{:S(2)}) collective-permute-start(bf16[512,128]{1,0:T(8,128)(2,1)S(1)} %pad_maximum_fusion.1.own_ref), channel_id=1, source_target_pairs={{0,8},{4,12},{8,16},{12,20},{16,24},{20,28},{1,9},{5,13},{9,17},{1... | collective-permute-start | bytes 393224 | tf_op jit(solution)/shard_map/ppermute | solution.py:255
  12.3 5.0 %collective-permute-start = (bf16[512,128]{1,0:T(8,128)(2,1)S(1)}, bf16[512,128]{1,0:T(8,128)(2,1)S(1)}, u32[]{:S(2)}, u32[]{:S(2)}) collective-permute-start(bf16[512,128]{1,0:T(8,128)(2,1)S(1)} %pad_maximum_fusion.1.own_ref), channel_id=1, source_target_pairs={{0,4},{4,0},{8,12},{12,8},{16,20},{20,16},{24,28},{28,24},{1,5},{5... | collective-permute-start | bytes 393224 | tf_op jit(solution)/shard_map/ppermute | solution.py:259
  17.4 9.6 %collective-permute-start.4 = (bf16[1536,128]{1,0:T(8,128)(2,1)S(1)}, bf16[1536,128]{1,0:T(8,128)(2,1)S(1)}, u32[]{:S(2)}, u32[]{:S(2)}) collective-permute-start(bf16[1536,128]{1,0:T(8,128)(2,1)S(1)} %pad_maximum_fusion), channel_id=1, source_target_pairs={{0,4},{4,0},{8,12},{12,8},{16,20},{20,16},{24,28},{28,24},{1,5},{5... | collective-permute-start | bytes 1179656 | tf_op jit(solution)/shard_map/ppermute | solution.py:259
  19.8 12.4 %copy-start = (bf16[256,8,128]{2,1,0:T(8,128)(2,1)S(1)}, bf16[256,8,128]{2,1,0:T(8,128)(2,1)}, u32[]{:S(2)}) copy-start(bf16[256,8,128]{2,1,0:T(8,128)(2,1)} %q_ref.1) | copy-start | bytes 1572868
  19.8 12.4 %all-to-all-start = ((bf16[64,4,1024]{2,0,1:T(8,128)(2,1)}), bf16[64,4,1024]{2,0,1:T(8,128)(2,1)S(1)}, u32[]{:S(2)}, u32[]{:S(2)}) async-start(bf16[64,4,1024]{2,0,1:T(8,128)(2,1)} %bitcast.19), calls=%async_computation | async-start | bytes 1048576 | tf_op jit(solution)/shard_map/all_to_all | solution.py:275
  23.5 8.7 %copy-start.1 = (s32[8]{0:T(128)S(1)}, s32[8]{0:T(128)}, u32[]{:S(2)}) copy-start(s32[8]{0:T(128)} %doc_ref.1) | copy-start | bytes 100
  40.7 16.5 %copy-start.2 = (f32[1024,256]{1,0:T(8,128)S(1)}, f32[1024,256]{1,0:T(8,128)}, u32[]{:S(2)}) copy-start(f32[1024,256]{1,0:T(8,128)} %get-tuple-element.20) | copy-start | bytes 3145732
  40.7 15.7 %collective-permute-start.5 = (bf16[1024,256]{1,0:T(8,128)(2,1)S(1)}, bf16[1024,256]{1,0:T(8,128)(2,1)S(1)}, u32[]{:S(2)}, u32[]{:S(2)}) collective-permute-start(bf16[1024,256]{1,0:T(8,128)(2,1)S(1)} %get-tuple-element.21), channel_id=1, source_target_pairs={{0,4},{4,0},{8,12},{12,8},{16,20},{20,16},{24,28},{28,24},{1,5},{5... | collective-permute-start | bytes 1572872 | tf_op jit(solution)/shard_map/ppermute | solution.py:259
  44.7 17.6 %all-to-all-start.1 = ((bf16[4,64,1024]{2,1,0:T(8,128)(2,1)}), bf16[4,64,1024]{2,1,0:T(8,128)(2,1)S(1)}, u32[]{:S(2)}, u32[]{:S(2)}) async-start(bf16[4,64,1024]{2,1,0:T(8,128)(2,1)} %bitcast.7), calls=%async_computation.1 | async-start | bytes 1048576 | tf_op jit(solution)/shard_map/all_to_all | solution.py:282
  56.4 0.8 copy-start.4
  58.4 30.3 %collective-permute-start.6 = (bf16[256,256]{1,0:T(8,128)(2,1)S(1)}, bf16[256,256]{1,0:T(8,128)(2,1)S(1)}, u32[]{:S(2)}, u32[]{:S(2)}) collective-permute-start(bf16[256,256]{1,0:T(8,128)(2,1)S(1)} %get-tuple-element.24), channel_id=1, source_target_pairs={{24,0},{28,4},{25,1},{29,5},{26,2},{30,6},{27,3},{31,7}} | collective-permute-start | bytes 393224 | tf_op jit(solution)/shard_map/ppermute | solution.py:255
  59.7 29.0 %collective-permute-start.8 = (bf16[256,256]{1,0:T(8,128)(2,1)S(1)}, bf16[256,256]{1,0:T(8,128)(2,1)S(1)}, u32[]{:S(2)}, u32[]{:S(2)}) collective-permute-start(bf16[256,256]{1,0:T(8,128)(2,1)S(1)} %get-tuple-element.25), channel_id=1, source_target_pairs={{8,0},{12,4},{16,8},{20,12},{24,16},{28,20},{9,1},{13,5},{17,9},{2... | collective-permute-start | bytes 393224 | tf_op jit(solution)/shard_map/ppermute | solution.py:255
  61.0 28.3 %collective-permute-start.7 = (bf16[256,256]{1,0:T(8,128)(2,1)S(1)}, bf16[256,256]{1,0:T(8,128)(2,1)S(1)}, u32[]{:S(2)}, u32[]{:S(2)}) collective-permute-start(bf16[256,256]{1,0:T(8,128)(2,1)S(1)} %get-tuple-element.26), channel_id=1, source_target_pairs={{16,0},{20,4},{24,8},{28,12},{17,1},{21,5},{25,9},{29,13},{18,2},{... | collective-permute-start | bytes 393224 | tf_op jit(solution)/shard_map/ppermute | solution.py:255
where the time goes:
time: 91.3 us; the launch traced here: 90 us
  waiting for transfers between devices  46.5 us (51%)
  starting transfers between devices  28.8 us (32%)
  Pallas kernels  8.47 us (9%)
  local copies, waits for them, and re-layouts  3.17 us (3%)
  other arithmetic  2.27 us (2%)
    ppermute x6, waiting for transfers between devices, shifted(): return lax.ppermute(block, 'ctx', pairs)  29.1 us
    ppermute x6, starting transfers between devices, shifted(): return lax.ppermute(block, 'ctx', pairs)  14.6 us
    ppermute x3, waiting for transfers between devices, exchanged(): return lax.ppermute(block, 'ctx', [(i, i ^ 1) for i in range(count)])  12.2 us
    pallas_call x1, Pallas kernels, attend(): pl.pallas_call(functools.partial(attention_kernel, back=back, heads=heads...  8.47 us
    ppermute x3, starting transfers between devices, exchanged(): return lax.ppermute(block, 'ctx', [(i, i ^ 1) for i in range(count)])  7.14 us
    all_to_all x1, waiting for transfers between devices, body(): lax.all_to_all(grad_attended, 'head', split_axis=1, concat_axis=0, tiled=...  5.22 us
    all_to_all x1, starting transfers between devices, body(): lax.all_to_all(grad_attended, 'head', split_axis=1, concat_axis=0, tiled=...  3.6 us
    all_to_all x1, starting transfers between devices, body(): lax.all_to_all(attended, 'head', split_axis=0, concat_axis=1, tiled=True)  3.47 us
  transfers between devices with their start and end apart: 11, of which 8 were waited for; matrix products, arithmetic and copies ran while one was open for 3% of the time, Pallas kernels for 0%

commit v1 on v0

v1 whole, which is shorter than its diff:
```python
import functools
import math

import jax
import jax.numpy as jnp
from jax import lax
from jax.experimental import pallas as pl
from jax.experimental.pallas import tpu as pltpu
from jax.sharding import PartitionSpec as P

DOC_MOST = 1792
NEG_FILL = -1e30
TILE = 256
CHUNK = 128
LOG2_E = 1.4426950408889634


def dot(a, b):
    return jnp.dot(a, b, preferred_element_type=jnp.float32)


def dot_nt(a, b):
    return lax.dot_general(a, b, (((1,), (1,)), ((), ())), preferred_element_type=jnp.float32)


def unit(size):
    rows = lax.broadcasted_iota(jnp.int32, (size, size), 0)
    return (rows == lax.broadcasted_iota(jnp.int32, (size, size), 1)).astype(jnp.bfloat16)


def twice(column):
    return jnp.concatenate([column, column], axis=1)


def attention_kernel(
    doc_ref,
    place_ref,
    q_ref,
    do_ref,
    own_ref,
    near_ref,
    far_ref,
    *refs,
    back,
    heads,
    width,
    scale,
):
    arrived = refs[:back]
    (o_ref, dq_ref, dmine_ref, dother_ref) = refs[back : back + 4]
    (
        q32,
        keys,
        values,
        q_rows,
        do_rows,
        q_cols,
        do_cols,
        scores,
        accum,
        dq_acc,
        top,
        delta,
        d_blocks,
    ) = refs[back + 4 :]
    tok = q_ref.shape[0]
    docs = doc_ref.shape[0]
    base = place_ref[0]
    own = place_ref[1]
    parity = place_ref[2]
    small = unit(width)
    ones = jnp.ones((width, width), jnp.bfloat16)

    values[:, width:] = jnp.ones_like(values[:, width:])
    for pair in range(back + 1):
        k = back - pair
        mine = own_ref if k == 0 else arrived[k - 1]
        for ref, first, place in (
            (mine, 0, 2 * pair + parity),
            (near_ref, 0, 2 * pair + 1 - parity)
            if k == 0
            else (far_ref, 2 * tok * (k - 1), 2 * pair + 1 - parity),
        ):
            at = pl.ds(pl.multiple_of(place * tok, tok), tok)
            keys[at, :] = ref[first : first + tok, :]
            values[at, 0:width] = ref[first + tok : first + 2 * tok, :]

    q32[...] = q_ref[...].astype(jnp.float32)
    d_blocks[...] = jnp.zeros_like(d_blocks)

    def chunk_step(chunk, carry):
        here = pl.ds(pl.multiple_of(chunk * CHUNK, CHUNK), CHUNK)
        for j in range(heads):
            part = pl.ds(j * CHUNK, CHUNK)
            q_rows[part, :] = q32[here, j, :].astype(jnp.bfloat16)
            do_rows[part, :] = do_ref[here, j * width : (j + 1) * width]
        q_cols[...] = dot_nt(small, q_rows[...]).astype(jnp.bfloat16)
        do_cols[...] = dot_nt(small, do_rows[...]).astype(jnp.bfloat16)
        top[...] = jnp.full_like(top, NEG_FILL)

        t_first = base + own * TILE + chunk * CHUNK
        t_last = t_first + CHUNK - 1
        t_col = t_first + lax.broadcasted_iota(jnp.int32, (CHUNK, width), 0)
        end = jnp.int32(0)
        start_first, start_last = jnp.int32(0), jnp.int32(0)
        start_col = jnp.zeros((CHUNK, width), jnp.int32)
        for i in range(docs):
            end = end + doc_ref[i]
            start_first = jnp.where(end <= t_first, end, start_first)
            start_last = jnp.where(end <= t_last, end, start_last)
            start_col = jnp.where(t_col >= end, end, start_col)
        low = jnp.maximum(start_first - base, 0) // TILE
        clear = jnp.clip((start_last - base + TILE - 1) // TILE, low, own)

        def score_tile(i, masked):
            at = pl.ds(pl.multiple_of(i * TILE, TILE), TILE)
            tile = dot_nt(q_rows[...], keys[at, :]) * (scale * LOG2_E)
            if masked:
                s_row = base + i * TILE + lax.broadcasted_iota(jnp.int32, (CHUNK, TILE), 1)
                live = (s_row >= twice(start_col)) & (s_row <= twice(t_col))
                tile = jnp.concatenate(
                    [
                        jnp.where(live, tile[j * CHUNK : (j + 1) * CHUNK], NEG_FILL)
                        for j in range(heads)
                    ],
                    axis=0,
                )
            scores[i] = tile
            top[...] = jnp.maximum(top[...], jnp.maximum(tile[:, :width], tile[:, width:]))

        def edge_step(n, carry):
            score_tile(jnp.where(n < clear - low, low + n, own), True)
            return carry

        def inner_step(i, carry):
            score_tile(i, False)
            return carry

        lax.fori_loop(0, clear - low + 1, edge_step, 0)
        lax.fori_loop(clear, own, inner_step, 0)
        top[...] = jnp.broadcast_to(jnp.max(top[...], axis=1, keepdims=True), top.shape)
        accum[...] = jnp.zeros_like(accum)

        def weigh_step(i, carry):
            at = pl.ds(pl.multiple_of(i * TILE, TILE), TILE)
            weights = jnp.exp2(scores[i] - twice(top[...])).astype(jnp.bfloat16)
            accum[...] += dot(weights, values[at, :])
            return carry

        lax.fori_loop(low, own + 1, weigh_step, 0)
        total = accum[:, width:]
        out = (accum[:, 0:width] / total).astype(jnp.bfloat16)
        for j in range(heads):
            o_ref[here, j * width : (j + 1) * width] = out[j * CHUNK : (j + 1) * CHUNK]
        top[...] = top[...] + jnp.log2(total)
        product = do_rows[...].astype(jnp.float32) * out.astype(jnp.float32)
        coarse = product.astype(jnp.bfloat16)
        fine = (product - coarse.astype(jnp.float32)).astype(jnp.bfloat16)
        delta[...] = dot(coarse, ones) + dot(fine, ones)
        dq_acc[...] = jnp.zeros_like(dq_acc)

        def back_step(i, carry):
            at = pl.ds(pl.multiple_of(i * TILE, TILE), TILE)
            probs = jnp.exp2(scores[i] - twice(top[...]))
            d_probs = dot_nt(do_rows[...], values[at, 0:width])
            d_scores = (probs * (d_probs - twice(delta[...]))).astype(jnp.bfloat16)
            dq_acc[...] += dot(d_scores, keys[at, :])
            d_blocks[i, 0:width, :] += dot(q_cols[...], d_scores)
            d_blocks[i, width:, :] += dot(do_cols[...], probs.astype(jnp.bfloat16))
            return carry

        lax.fori_loop(low, own + 1, back_step, 0)
        for j in range(heads):
            q32[here, j, :] = dq_acc[j * CHUNK : (j + 1) * CHUNK, :] * scale
        return carry

    lax.fori_loop(0, tok // CHUNK, chunk_step, 0)
    dq_ref[...] = q32[...].astype(jnp.bfloat16)
    for pair in range(back + 1):
        mine, other = 2 * pair + parity, 2 * pair + 1 - parity
        dmine_ref[pair, 0:width, :] = d_blocks[mine, 0:width, :] * scale
        dmine_ref[pair, width:, :] = d_blocks[mine, width:, :]
        dother_ref[pair, 0:width, :] = (d_blocks[other, 0:width, :] * scale).astype(jnp.bfloat16)
        dother_ref[pair, width:, :] = d_blocks[other, width:, :].astype(jnp.bfloat16)


def attend(doc_lengths, place, queries, grad_rows, own, near, far, arrived):
    tok, heads, width = queries.shape
    back = len(arrived)
    tiles = 2 * (back + 1)
    span = tiles * tok
    rows = heads * CHUNK
    vmem = pl.BlockSpec(memory_space=pltpu.VMEM)
    smem = pl.BlockSpec(memory_space=pltpu.SMEM)
    return pl.pallas_call(
        functools.partial(
            attention_kernel,
            back=back,
            heads=heads,
            width=width,
            scale=1.0 / math.sqrt(width),
        ),
        out_shape=(
            jax.ShapeDtypeStruct((tok, heads * width), jnp.bfloat16),
            jax.ShapeDtypeStruct((tok, heads, width), jnp.bfloat16),
            jax.ShapeDtypeStruct((back + 1, 2 * width, tok), jnp.float32),
            jax.ShapeDtypeStruct((back + 1, 2 * width, tok), jnp.bfloat16),
        ),
        in_specs=[smem, smem] + [vmem] * (5 + back),
        out_specs=(vmem, vmem, vmem, vmem),
        scratch_shapes=[
            pltpu.VMEM((tok, heads, width), jnp.float32),
            pltpu.VMEM((span, width), jnp.bfloat16),
            pltpu.VMEM((span, 2 * width), jnp.bfloat16),
            pltpu.VMEM((rows, width), jnp.bfloat16),
            pltpu.VMEM((rows, width), jnp.bfloat16),
            pltpu.VMEM((width, rows), jnp.bfloat16),
            pltpu.VMEM((width, rows), jnp.bfloat16),
            pltpu.VMEM((tiles, rows, TILE), jnp.float32),
            pltpu.VMEM((rows, 2 * width), jnp.float32),
            pltpu.VMEM((rows, width), jnp.float32),
            pltpu.VMEM((rows, width), jnp.float32),
            pltpu.VMEM((rows, width), jnp.float32),
            pltpu.VMEM((tiles, 2 * width, tok), jnp.float32),
        ],
        compiler_params=pltpu.CompilerParams(vmem_limit_bytes=40 * 1024 * 1024),
        cost_estimate=pl.CostEstimate(
            flops=14 * tok * heads * width * span,
            bytes_accessed=4 * tok * heads * width * 2 + 4 * span * width * 2,
            transcendentals=tok * heads * span,
        ),
        name="attention",
    )(doc_lengths, place, queries, grad_rows, own, near, far, *arrived)


def finish_kernel(own_ref, *refs):
    arrived = refs[:-2]
    dk_ref, dv_ref = refs[-2:]
    total = own_ref[...]
    for ref in arrived:
        total = total + ref[...].astype(jnp.float32)
    total = total.astype(jnp.bfloat16)
    width = dk_ref.shape[1]
    large = unit(dk_ref.shape[0])
    dk_ref[...] = dot_nt(large, total[:width]).astype(jnp.bfloat16)
    dv_ref[...] = dot_nt(large, total[width:]).astype(jnp.bfloat16)


def finish(own_part, arrived):
    both, tok = own_part.shape
    vmem = pl.BlockSpec(memory_space=pltpu.VMEM)
    shape = jax.ShapeDtypeStruct((tok, both // 2), jnp.bfloat16)
    return pl.pallas_call(
        finish_kernel,
        out_shape=(shape, shape),
        in_specs=[vmem] * (1 + len(arrived)),
        out_specs=(vmem, vmem),
        name="finish",
    )(own_part, *arrived)


def shifted(block, by, count):
    pairs = [(i, i + by) for i in range(count) if 0 <= i + by < count]
    return lax.ppermute(block, "ctx", pairs)


def exchanged(block, count):
    return lax.ppermute(block, "ctx", [(i, i ^ 1) for i in range(count)])


def body(queries, key_states, value_states, doc_lengths, grad_attended):
    tok, heads, width = queries.shape
    count = lax.axis_size("ctx")
    ctx = lax.axis_index("ctx")
    reach = min((DOC_MOST + tok - 2) // tok, count - 1)
    back = min((reach + 1) // 2, count // 2 - 1)
    own = jnp.concatenate(
        [key_states.reshape(tok, width), value_states.reshape(tok, width)], axis=0
    )
    near = exchanged(own, count)
    arrived = [shifted(own, 2 * k, count) for k in range(1, back + 1)]
    near, arrived, grad_attended = lax.optimization_barrier((near, arrived, grad_attended))
    far = exchanged(jnp.concatenate(arrived, axis=0), count)
    grad_rows = lax.all_to_all(grad_attended, "head", split_axis=1, concat_axis=0, tiled=True)
    parity = ctx % 2
    place = jnp.stack([(ctx - parity - 2 * back) * tok, 2 * back + parity, parity])
    attended, grad_queries, d_mine, d_other = attend(
        doc_lengths, place.astype(jnp.int32), queries, grad_rows, own, near, far, arrived
    )
    d_near = exchanged(d_other, count)
    attended = lax.all_to_all(attended, "head", split_axis=0, concat_axis=1, tiled=True)
    total = d_mine + d_near.astype(jnp.float32)
    arrived = [
        shifted(total[back - k].astype(jnp.bfloat16), -2 * k, count) for k in range(back, 0, -1)
    ]
    grad_keys, grad_values = finish(total[back], arrived)
    grad_keys = grad_keys.reshape(tok, 1, width)
    grad_values = grad_values.reshape(tok, 1, width)
    return attended, grad_queries, grad_keys, grad_values


def solution(mesh):
    in_specs = (
        P("ctx", "head", None),
        P("ctx", "head", None),
        P("ctx", "head", None),
        P(),
        P(("ctx", "head"), None),
    )
    out_specs = (
        P(("ctx", "head"), None),
        P("ctx", "head", None),
        P("ctx", "head", None),
        P("ctx", "head", None),
    )
    return jax.shard_map(body, mesh=mesh, in_specs=in_specs, out_specs=out_specs, check_vma=False)
```

time: 91.3 us -> 89.5 us (0.980); the launches traced: 90 us -> 89.2 us
  blocking collectives: 0 us -> 11.2 us
  waiting for transfers between devices: 46.5 us -> 37.4 us
  starting transfers between devices: 28.8 us -> 24.6 us
  Pallas kernels: 8.47 us -> 10.3 us
  other arithmetic: 2.27 us -> 1.19 us
    all_to_all x0 -> x1, blocking collectives: none -> 11.2 us  [body(): lax.all_to_all(attended, 'head', split_axis=0, concat_axis=1, tiled=True)]
    ppermute x3, waiting for transfers between devices: 12.2 us -> 3.93 us  [exchanged(): return lax.ppermute(block, 'ctx', [(i, i ^ 1) for i in range(count)])]
    all_to_all x1 -> x0, starting transfers between devices: 3.47 us -> none  [body(): lax.all_to_all(attended, 'head', split_axis=0, concat_axis=1, tiled=True)]
    pallas_call x0 -> x1, Pallas kernels: none -> 2.02 us  [finish(): pl.pallas_call(finish_kernel, out_shape=(shape, shape), in_specs=[vmem] *...]
    another operation x1, other arithmetic: 1.17 us -> 0.15 us
  transfers between devices with their start and end apart: 11 -> 10, of which waited for: 8 -> 7; matrix products, arithmetic and copies ran while one was open for 3% -> 3% of each run, Pallas kernels for 0% -> 0%
where the time goes in v1:
time: 89.5 us; the launch traced here: 89.2 us
  waiting for transfers between devices  37.4 us (42%)
  starting transfers between devices  24.6 us (27%)
  blocking collectives  11.2 us (13%)
  Pallas kernels  10.3 us (12%)
  local copies, waits for them, and re-layouts  3.71 us (4%)
  other arithmetic  1.19 us (1%)
    ppermute x6, waiting for transfers between devices, shifted(): return lax.ppermute(block, 'ctx', pairs)  28.3 us
    ppermute x6, starting transfers between devices, shifted(): return lax.ppermute(block, 'ctx', pairs)  14.6 us
    all_to_all x1, blocking collectives, body(): lax.all_to_all(attended, 'head', split_axis=0, concat_axis=1, tiled=True)  11.2 us
    pallas_call x1, Pallas kernels, attend(): pl.pallas_call(functools.partial(attention_kernel, back=back, heads=heads...  8.24 us
    ppermute x3, starting transfers between devices, exchanged(): return lax.ppermute(block, 'ctx', [(i, i ^ 1) for i in range(count)])  6.37 us
    all_to_all x1, waiting for transfers between devices, body(): lax.all_to_all(grad_attended, 'head', split_axis=1, concat_axis=0, tiled=...  5.22 us
    ppermute x3, waiting for transfers between devices, exchanged(): return lax.ppermute(block, 'ctx', [(i, i ^ 1) for i in range(count)])  3.93 us
    all_to_all x1, starting transfers between devices, body(): lax.all_to_all(grad_attended, 'head', split_axis=1, concat_axis=0, tiled=...  3.6 us
  transfers between devices with their start and end apart: 10, of which 7 were waited for; matrix products, arithmetic and copies ran while one was open for 3% of the time, Pallas kernels for 0%

profile of v1, /device:TPU:0, one launch (start us, length us, event | category | flops | bytes accessed | tf_op | source)
XLA Modules:
  0.0 89.2 jit_solution(10614116897201216727)
XLA Ops:
  0.6 0.0 copy-start.2
  0.6 0.9 %pad_maximum_fusion.1.own_ref = bf16[512,128]{1,0:T(8,128)(2,1)S(1)} fusion(bf16[256,128]{1,0:T(8,128)(2,1)} %bitcast.31, bf16[256,128]{1,0:T(8,128)(2,1)} %bitcast.32), kind=kLoop, calls=%fused_computation.7 | loop fusion | flops 262144 | bytes 262144 | tf_op jit(solution)/shard_map/concatenate | solution.py:277
  1.6 7.0 %collective-permute-start.3 = (bf16[512,128]{1,0:T(8,128)(2,1)S(1)}, bf16[512,128]{1,0:T(8,128)(2,1)S(1)}, u32[]{:S(2)}, u32[]{:S(2)}) collective-permute-start(bf16[512,128]{1,0:T(8,128)(2,1)S(1)} %pad_maximum_fusion.1.own_ref), channel_id=1, source_target_pairs={{0,24},{4,28},{1,25},{5,29},{2,26},{6,30},{3,27},{7,31}} | collective-permute-start | bytes 393224 | tf_op jit(solution)/shard_map/ppermute | solution.py:264
  8.6 1.3 %collective-permute-start.2 = (bf16[512,128]{1,0:T(8,128)(2,1)S(1)}, bf16[512,128]{1,0:T(8,128)(2,1)S(1)}, u32[]{:S(2)}, u32[]{:S(2)}) collective-permute-start(bf16[512,128]{1,0:T(8,128)(2,1)S(1)} %pad_maximum_fusion.1.own_ref), channel_id=1, source_target_pairs={{0,16},{4,20},{8,24},{12,28},{1,17},{5,21},{9,25},{13,29},{2,18},{... | collective-permute-start | bytes 393224 | tf_op jit(solution)/shard_map/ppermute | solution.py:264
  9.9 2.5 %collective-permute-start.1 = (bf16[512,128]{1,0:T(8,128)(2,1)S(1)}, bf16[512,128]{1,0:T(8,128)(2,1)S(1)}, u32[]{:S(2)}, u32[]{:S(2)}) collective-permute-start(bf16[512,128]{1,0:T(8,128)(2,1)S(1)} %pad_maximum_fusion.1.own_ref), channel_id=1, source_target_pairs={{0,8},{4,12},{8,16},{12,20},{16,24},{20,28},{1,9},{5,13},{9,17},{1... | collective-permute-start | bytes 393224 | tf_op jit(solution)/shard_map/ppermute | solution.py:264
  12.3 1.6 %collective-permute-start = (bf16[512,128]{1,0:T(8,128)(2,1)S(1)}, bf16[512,128]{1,0:T(8,128)(2,1)S(1)}, u32[]{:S(2)}, u32[]{:S(2)}) collective-permute-start(bf16[512,128]{1,0:T(8,128)(2,1)S(1)} %pad_maximum_fusion.1.own_ref), channel_id=1, source_target_pairs={{0,4},{4,0},{8,12},{12,8},{16,20},{20,16},{24,28},{28,24},{1,5},{5... | collective-permute-start | bytes 393224 | tf_op jit(solution)/shard_map/ppermute | solution.py:268
  13.9 0.0 collective-permute-done.3.refs_2_
  13.9 1.4 %collective-permute-done.2.refs_1_ = bf16[512,128]{1,0:T(8,128)(2,1)S(1)} collective-permute-done((bf16[512,128]{1,0:T(8,128)(2,1)S(1)}, bf16[512,128]{1,0:T(8,128)(2,1)S(1)}, u32[]{:S(2)}, u32[]{:S(2)}) %collective-permute-start.2) | collective-permute-done | bytes 131104 | tf_op jit(solution)/shard_map/ppermute | solution.py:264
  15.3 1.7 %collective-permute-done.1.refs_0_ = bf16[512,128]{1,0:T(8,128)(2,1)S(1)} collective-permute-done((bf16[512,128]{1,0:T(8,128)(2,1)S(1)}, bf16[512,128]{1,0:T(8,128)(2,1)S(1)}, u32[]{:S(2)}, u32[]{:S(2)}) %collective-permute-start.1) | collective-permute-done | bytes 131104 | tf_op jit(solution)/shard_map/ppermute | solution.py:264
  16.9 0.4 collective-permute-done.near_ref
  17.4 1.6 %collective-permute-start.4 = (bf16[1536,128]{1,0:T(8,128)(2,1)S(1)}, bf16[1536,128]{1,0:T(8,128)(2,1)S(1)}, u32[]{:S(2)}, u32[]{:S(2)}) collective-permute-start(bf16[1536,128]{1,0:T(8,128)(2,1)S(1)} %pad_maximum_fusion), channel_id=1, source_target_pairs={{0,4},{4,0},{8,12},{12,8},{16,20},{20,16},{24,28},{28,24},{1,5},{5... | collective-permute-start | bytes 1179656 | tf_op jit(solution)/shard_map/ppermute | solution.py:268
  19.0 0.0 copy-done.2
  19.0 0.8 copy.14
  19.8 0.0 copy-start
  19.8 3.6 %all-to-all-start = ((bf16[64,4,1024]{2,0,1:T(8,128)(2,1)}), bf16[64,4,1024]{2,0,1:T(8,128)(2,1)S(1)}, u32[]{:S(2)}, u32[]{:S(2)}) async-start(bf16[64,4,1024]{2,0,1:T(8,128)(2,1)} %bitcast.25), calls=%async_computation | async-start | bytes 1048576 | tf_op jit(solution)/shard_map/all_to_all | solution.py:284
  23.4 0.1 pad_add_fusion.place_ref
  23.5 0.0 copy-start.1
  23.5 3.5 %collective-permute-done.4.far_ref = bf16[1536,128]{1,0:T(8,128)(2,1)S(1)} collective-permute-done((bf16[1536,128]{1,0:T(8,128)(2,1)S(1)}, bf16[1536,128]{1,0:T(8,128)(2,1)S(1)}, u32[]{:S(2)}, u32[]{:S(2)}) %collective-permute-start.4) | collective-permute-done | bytes 393248 | tf_op jit(solution)/shard_map/ppermute | solution.py:268
  27.0 5.2 %all-to-all-done = bf16[64,4,1024]{2,0,1:T(8,128)(2,1)S(1)} async-done(((bf16[64,4,1024]{2,0,1:T(8,128)(2,1)}), bf16[64,4,1024]{2,0,1:T(8,128)(2,1)S(1)}, u32[]{:S(2)}, u32[]{:S(2)}) %all-to-all-start) | async-done | bytes 524320 | tf_op jit(solution)/shard_map/all_to_all | solution.py:284
  32.2 0.0 copy-done
  32.2 0.0 copy-done.1
  32.2 8.2 %attention.1 = (bf16[256,1024]{1,0:T(8,128)(2,1)S(1)}, bf16[256,8,128]{2,1,0:T(8,128)(2,1)}, f32[4,256,256]{2,1,0:T(8,128)S(1)}, bf16[4,256,256]{2,1,0:T(8,128)(2,1)S(1)}) custom-call(s32[8]{0:T(128)S(1)} %copy-done.1, s32[3]{0:T(128)S(1)} %pad_add_fusion.place_ref, bf16[256,8,128]{2,1,0:T(8,128)(2,1)S(1)} %copy-done, bf16[256,1024]{1,0:T(8,128)(2,1)S(1)} %bitcast.26, ...), custom_call_target="tpu_custom_call" | custom-call | flops 7516192768 | bytes 4194304 | tf_op jit(solution)/shard_map/attention/pallas_call | solution.py:195
  40.5 3.2 %collective-permute-start.5 = (bf16[4,256,256]{2,1,0:T(8,128)(2,1)S(1)}, bf16[4,256,256]{2,1,0:T(8,128)(2,1)S(1)}, u32[]{:S(2)}, u32[]{:S(2)}) collective-permute-start(bf16[4,256,256]{2,1,0:T(8,128)(2,1)S(1)} %get-tuple-element.23), channel_id=1, source_target_pairs={{0,4},{4,0},{8,12},{12,8},{16,20},{20,16},{24,28},{28,24},{1,5},{5... | collective-permute-start | bytes 1572872 | tf_op jit(solution)/shard_map/ppermute | solution.py:268
  43.7 11.2 %all_to_all.38 = bf16[4,64,1024]{2,1,0:T(8,128)(2,1)S(1)} all-to-all(bf16[4,64,1024]{2,1,0:T(8,128)(2,1)S(1)} %bitcast.27), channel_id=1, replica_groups=mesh['ctx'=8,'head'=4] {'head'}, dimensions={0} | all-to-all | bytes 1048576 | tf_op jit(solution)/shard_map/all_to_all | solution.py:291
  54.9 0.8 copy.12
  55.7 0.0 collective-permute-done.5
  55.8 0.2 fusion
  55.9 1.3 %collective-permute-start.8 = (bf16[256,256]{1,0:T(8,128)(2,1)S(1)}, bf16[256,256]{1,0:T(8,128)(2,1)S(1)}, u32[]{:S(2)}, u32[]{:S(2)}) collective-permute-start(bf16[256,256]{1,0:T(8,128)(2,1)S(1)} %get-tuple-element.28), channel_id=1, source_target_pairs={{8,0},{12,4},{16,8},{20,12},{24,16},{28,20},{9,1},{13,5},{17,9},{2... | collective-permute-start | bytes 393224 | tf_op jit(solution)/shard_map/ppermute | solution.py:264
  57.2 1.3 %collective-permute-start.7 = (bf16[256,256]{1,0:T(8,128)(2,1)S(1)}, bf16[256,256]{1,0:T(8,128)(2,1)S(1)}, u32[]{:S(2)}, u32[]{:S(2)}) collective-permute-start(bf16[256,256]{1,0:T(8,128)(2,1)S(1)} %get-tuple-element.29), channel_id=1, source_target_pairs={{16,0},{20,4},{24,8},{28,12},{17,1},{21,5},{25,9},{29,13},{18,2},{... | collective-permute-start | bytes 393224 | tf_op jit(solution)/shard_map/ppermute | solution.py:264
  58.5 1.3 %collective-permute-start.6 = (bf16[256,256]{1,0:T(8,128)(2,1)S(1)}, bf16[256,256]{1,0:T(8,128)(2,1)S(1)}, u32[]{:S(2)}, u32[]{:S(2)}) collective-permute-start(bf16[256,256]{1,0:T(8,128)(2,1)S(1)} %get-tuple-element.30), channel_id=1, source_target_pairs={{24,0},{28,4},{25,1},{29,5},{26,2},{30,6},{27,3},{31,7}} | collective-permute-start | bytes 393224 | tf_op jit(solution)/shard_map/ppermute | solution.py:264
  59.8 0.7 slice_bitcast_fusion.own_ref
  60.6 9.7 %collective-permute-done.8.refs_2_ = bf16[256,256]{1,0:T(8,128)(2,1)S(1)} collective-permute-done((bf16[256,256]{1,0:T(8,128)(2,1)S(1)}, bf16[256,256]{1,0:T(8,128)(2,1)S(1)}, u32[]{:S(2)}, u32[]{:S(2)}) %collective-permute-start.8) | collective-permute-done | bytes 131104 | tf_op jit(solution)/shard_map/ppermute | solution.py:264
  70.2 0.0 copy-start.3
  70.2 15.6 %collective-permute-done.7.refs_1_ = bf16[256,256]{1,0:T(8,128)(2,1)S(1)} collective-permute-done((bf16[256,256]{1,0:T(8,128)(2,1)S(1)}, bf16[256,256]{1,0:T(8,128)(2,1)S(1)}, u32[]{:S(2)}, u32[]{:S(2)}) %collective-permute-start.7) | collective-permute-done | bytes 131104 | tf_op jit(solution)/shard_map/ppermute | solution.py:264
  85.8 0.0 copy-start.4
  85.8 0.0 collective-permute-done.6.refs_0_
  85.8 0.0 copy-done.3
  85.8 0.6 copy-done.4
  86.5 0.0 copy-start.5
  86.5 0.6 copy-done.5
  87.1 2.0 %finish.1 = (bf16[256,128]{1,0:T(8,128)(2,1)}, bf16[256,128]{1,0:T(8,128)(2,1)}) custom-call(f32[256,256]{1,0:T(8,128)} %slice_bitcast_fusion.own_ref, bf16[256,256]{1,0:T(8,128)(2,1)} %copy-done.5, bf16[256,256]{1,0:T(8,128)(2,1)} %copy-done.4, bf16[256,256]{1,0:T(8,128)(2,1)} %copy-done.3), custom_call_target="tpu_custom_call" | custom-call | tf_op jit(solution)/shard_map/finish/pallas_call | solution.py:253
  (2 shorter events, 0.1 us)
Async XLA Ops:
  0.6 18.4 %copy-start.2 = (bf16[64,4096]{1,0:T(8,128)(2,1)S(1)}, bf16[64,4096]{1,0:T(8,128)(2,1)}, u32[]{:S(2)}) copy-start(bf16[64,4096]{1,0:T(8,128)(2,1)} %param.9) | copy-start | bytes 1572868
  1.6 12.3 %collective-permute-start.3 = (bf16[512,128]{1,0:T(8,128)(2,1)S(1)}, bf16[512,128]{1,0:T(8,128)(2,1)S(1)}, u32[]{:S(2)}, u32[]{:S(2)}) collective-permute-start(bf16[512,128]{1,0:T(8,128)(2,1)S(1)} %pad_maximum_fusion.1.own_ref), channel_id=1, source_target_pairs={{0,24},{4,28},{1,25},{5,29},{2,26},{6,30},{3,27},{7,31}} | collective-permute-start | bytes 393224 | tf_op jit(solution)/shard_map/ppermute | solution.py:264
  8.6 6.7 %collective-permute-start.2 = (bf16[512,128]{1,0:T(8,128)(2,1)S(1)}, bf16[512,128]{1,0:T(8,128)(2,1)S(1)}, u32[]{:S(2)}, u32[]{:S(2)}) collective-permute-start(bf16[512,128]{1,0:T(8,128)(2,1)S(1)} %pad_maximum_fusion.1.own_ref), channel_id=1, source_target_pairs={{0,16},{4,20},{8,24},{12,28},{1,17},{5,21},{9,25},{13,29},{2,18},{... | collective-permute-start | bytes 393224 | tf_op jit(solution)/shard_map/ppermute | solution.py:264
  9.9 7.1 %collective-permute-start.1 = (bf16[512,128]{1,0:T(8,128)(2,1)S(1)}, bf16[512,128]{1,0:T(8,128)(2,1)S(1)}, u32[]{:S(2)}, u32[]{:S(2)}) collective-permute-start(bf16[512,128]{1,0:T(8,128)(2,1)S(1)} %pad_maximum_fusion.1.own_ref), channel_id=1, source_target_pairs={{0,8},{4,12},{8,16},{12,20},{16,24},{20,28},{1,9},{5,13},{9,17},{1... | collective-permute-start | bytes 393224 | tf_op jit(solution)/shard_map/ppermute | solution.py:264
  12.3 5.0 %collective-permute-start = (bf16[512,128]{1,0:T(8,128)(2,1)S(1)}, bf16[512,128]{1,0:T(8,128)(2,1)S(1)}, u32[]{:S(2)}, u32[]{:S(2)}) collective-permute-start(bf16[512,128]{1,0:T(8,128)(2,1)S(1)} %pad_maximum_fusion.1.own_ref), channel_id=1, source_target_pairs={{0,4},{4,0},{8,12},{12,8},{16,20},{20,16},{24,28},{28,24},{1,5},{5... | collective-permute-start | bytes 393224 | tf_op jit(solution)/shard_map/ppermute | solution.py:268
  17.4 9.6 %collective-permute-start.4 = (bf16[1536,128]{1,0:T(8,128)(2,1)S(1)}, bf16[1536,128]{1,0:T(8,128)(2,1)S(1)}, u32[]{:S(2)}, u32[]{:S(2)}) collective-permute-start(bf16[1536,128]{1,0:T(8,128)(2,1)S(1)} %pad_maximum_fusion), channel_id=1, source_target_pairs={{0,4},{4,0},{8,12},{12,8},{16,20},{20,16},{24,28},{28,24},{1,5},{5... | collective-permute-start | bytes 1179656 | tf_op jit(solution)/shard_map/ppermute | solution.py:268
  19.8 12.4 %copy-start = (bf16[256,8,128]{2,1,0:T(8,128)(2,1)S(1)}, bf16[256,8,128]{2,1,0:T(8,128)(2,1)}, u32[]{:S(2)}) copy-start(bf16[256,8,128]{2,1,0:T(8,128)(2,1)} %q_ref.1) | copy-start | bytes 1572868
  19.8 12.4 %all-to-all-start = ((bf16[64,4,1024]{2,0,1:T(8,128)(2,1)}), bf16[64,4,1024]{2,0,1:T(8,128)(2,1)S(1)}, u32[]{:S(2)}, u32[]{:S(2)}) async-start(bf16[64,4,1024]{2,0,1:T(8,128)(2,1)} %bitcast.25), calls=%async_computation | async-start | bytes 1048576 | tf_op jit(solution)/shard_map/all_to_all | solution.py:284
  23.5 8.7 %copy-start.1 = (s32[8]{0:T(128)S(1)}, s32[8]{0:T(128)}, u32[]{:S(2)}) copy-start(s32[8]{0:T(128)} %doc_ref.1) | copy-start | bytes 100
  40.5 15.3 %collective-permute-start.5 = (bf16[4,256,256]{2,1,0:T(8,128)(2,1)S(1)}, bf16[4,256,256]{2,1,0:T(8,128)(2,1)S(1)}, u32[]{:S(2)}, u32[]{:S(2)}) collective-permute-start(bf16[4,256,256]{2,1,0:T(8,128)(2,1)S(1)} %get-tuple-element.23), channel_id=1, source_target_pairs={{0,4},{4,0},{8,12},{12,8},{16,20},{20,16},{24,28},{28,24},{1,5},{5... | collective-permute-start | bytes 1572872 | tf_op jit(solution)/shard_map/ppermute | solution.py:268
  55.9 14.3 %collective-permute-start.8 = (bf16[256,256]{1,0:T(8,128)(2,1)S(1)}, bf16[256,256]{1,0:T(8,128)(2,1)S(1)}, u32[]{:S(2)}, u32[]{:S(2)}) collective-permute-start(bf16[256,256]{1,0:T(8,128)(2,1)S(1)} %get-tuple-element.28), channel_id=1, source_target_pairs={{8,0},{12,4},{16,8},{20,12},{24,16},{28,20},{9,1},{13,5},{17,9},{2... | collective-permute-start | bytes 393224 | tf_op jit(solution)/shard_map/ppermute | solution.py:264
  57.2 28.6 %collective-permute-start.7 = (bf16[256,256]{1,0:T(8,128)(2,1)S(1)}, bf16[256,256]{1,0:T(8,128)(2,1)S(1)}, u32[]{:S(2)}, u32[]{:S(2)}) collective-permute-start(bf16[256,256]{1,0:T(8,128)(2,1)S(1)} %get-tuple-element.29), channel_id=1, source_target_pairs={{16,0},{20,4},{24,8},{28,12},{17,1},{21,5},{25,9},{29,13},{18,2},{... | collective-permute-start | bytes 393224 | tf_op jit(solution)/shard_map/ppermute | solution.py:264
  58.5 27.3 %collective-permute-start.6 = (bf16[256,256]{1,0:T(8,128)(2,1)S(1)}, bf16[256,256]{1,0:T(8,128)(2,1)S(1)}, u32[]{:S(2)}, u32[]{:S(2)}) collective-permute-start(bf16[256,256]{1,0:T(8,128)(2,1)S(1)} %get-tuple-element.30), channel_id=1, source_target_pairs={{24,0},{28,4},{25,1},{29,5},{26,2},{30,6},{27,3},{31,7}} | collective-permute-start | bytes 393224 | tf_op jit(solution)/shard_map/ppermute | solution.py:264
  70.2 15.6 %copy-start.3 = (bf16[256,256]{1,0:T(8,128)(2,1)}, bf16[256,256]{1,0:T(8,128)(2,1)S(1)}, u32[]{:S(2)}) copy-start(bf16[256,256]{1,0:T(8,128)(2,1)S(1)} %collective-permute-done.8.refs_2_) | copy-start | bytes 393220
  85.8 0.7 copy-start.4
  86.5 0.6 copy-start.5

commit v2 on v1

--- a/solution.py
+++ b/solution.py
@@ -36,19 +36,26 @@
     doc_ref,
     place_ref,
     q_ref,
-    do_ref,
     own_ref,
     near_ref,
-    far_ref,
     *refs,
     back,
+    ranks,
     heads,
     width,
     scale,
 ):
-    arrived = refs[:back]
-    (o_ref, dq_ref, dmine_ref, dother_ref) = refs[back : back + 4]
+    arrived, far, refs = refs[:back], refs[back : 2 * back], refs[2 * back :]
+    grad_parts, refs = refs[:ranks], refs[ranks:]
+    out_parts, refs = refs[:ranks], refs[ranks:]
     (
+        dq_ref,
+        mine_first_ref,
+        mine_last_ref,
+        other_first_ref,
+        other_last_ref,
+        do_ref,
+        o_ref,
         q32,
         keys,
         values,
@@ -62,28 +69,28 @@
         top,
         delta,
         d_blocks,
-    ) = refs[back + 4 :]
+    ) = refs
     tok = q_ref.shape[0]
+    part_rows = tok // ranks
     docs = doc_ref.shape[0]
     base = place_ref[0]
     own = place_ref[1]
     parity = place_ref[2]
+    rank = place_ref[3]
     small = unit(width)
     ones = jnp.ones((width, width), jnp.bfloat16)
 
     values[:, width:] = jnp.ones_like(values[:, width:])
     for pair in range(back + 1):
         k = back - pair
-        mine = own_ref if k == 0 else arrived[k - 1]
-        for ref, first, place in (
-            (mine, 0, 2 * pair + parity),
-            (near_ref, 0, 2 * pair + 1 - parity)
-            if k == 0
-            else (far_ref, 2 * tok * (k - 1), 2 * pair + 1 - parity),
-        ):
+        mine, other = (own_ref, near_ref) if k == 0 else (arrived[k - 1], far[k - 1])
+        for ref, place in ((mine, 2 * pair + parity), (other, 2 * pair + 1 - parity)):
             at = pl.ds(pl.multiple_of(place * tok, tok), tok)
-            keys[at, :] = ref[first : first + tok, :]
-            values[at, 0:width] = ref[first + tok : first + 2 * tok, :]
+            keys[at, :] = ref[0:tok, :]
+            values[at, 0:width] = ref[tok:, :]
+    for k in range(ranks):
+        at = pl.ds(pl.multiple_of((rank ^ k) * part_rows, part_rows), part_rows)
+        do_ref[at, :] = grad_parts[k][...]
 
     q32[...] = q_ref[...].astype(jnp.float32)
     d_blocks[...] = jnp.zeros_like(d_blocks)
@@ -175,40 +182,57 @@
         return carry
 
     lax.fori_loop(0, tok // CHUNK, chunk_step, 0)
+    for k in range(ranks):
+        at = pl.ds(pl.multiple_of((rank ^ k) * part_rows, part_rows), part_rows)
+        out_parts[k][...] = o_ref[at, :]
     dq_ref[...] = q32[...].astype(jnp.bfloat16)
     for pair in range(back + 1):
         mine, other = 2 * pair + parity, 2 * pair + 1 - parity
-        dmine_ref[pair, 0:width, :] = d_blocks[mine, 0:width, :] * scale
-        dmine_ref[pair, width:, :] = d_blocks[mine, width:, :]
-        dother_ref[pair, 0:width, :] = (d_blocks[other, 0:width, :] * scale).astype(jnp.bfloat16)
-        dother_ref[pair, width:, :] = d_blocks[other, width:, :].astype(jnp.bfloat16)
-
-
-def attend(doc_lengths, place, queries, grad_rows, own, near, far, arrived):
+        first = mine_first_ref.shape[0]
+        early = pair < first
+        to = pair if early else pair - first
+        ref = mine_first_ref if early else mine_last_ref
+        ref[to, 0:width, :] = d_blocks[mine, 0:width, :] * scale
+        ref[to, width:, :] = d_blocks[mine, width:, :]
+        ref = other_first_ref if early else other_last_ref
+        ref[to, 0:width, :] = (d_blocks[other, 0:width, :] * scale).astype(jnp.bfloat16)
+        ref[to, width:, :] = d_blocks[other, width:, :].astype(jnp.bfloat16)
+
+
+def attend(doc_lengths, place, queries, own, near, arrived, far, grad_parts):
     tok, heads, width = queries.shape
     back = len(arrived)
+    ranks = len(grad_parts)
+    first = (back + 1) // 2
     tiles = 2 * (back + 1)
     span = tiles * tok
     rows = heads * CHUNK
     vmem = pl.BlockSpec(memory_space=pltpu.VMEM)
     smem = pl.BlockSpec(memory_space=pltpu.SMEM)
+    out_part = jax.ShapeDtypeStruct((tok // ranks, heads * width), jnp.bfloat16)
     return pl.pallas_call(
         functools.partial(
             attention_kernel,
             back=back,
+            ranks=ranks,
             heads=heads,
             width=width,
             scale=1.0 / math.sqrt(width),
         ),
-        out_shape=(
-            jax.ShapeDtypeStruct((tok, heads * width), jnp.bfloat16),
+        out_shape=[out_part] * ranks
+        + [
             jax.ShapeDtypeStruct((tok, heads, width), jnp.bfloat16),
-            jax.ShapeDtypeStruct((back + 1, 2 * width, tok), jnp.float32),
-            jax.ShapeDtypeStruct((back + 1, 2 * width, tok), jnp.bfloat16),
-        ),
-        in_specs=[smem, smem] + [vmem] * (5 + back),
-        out_specs=(vmem, vmem, vmem, vmem),
+        ]
+        + [
+            jax.ShapeDtypeStruct((size, 2 * width, tok), dtype)
+            for dtype in (jnp.float32, jnp.bfloat16)
+            for size in (first, back + 1 - first)
+        ],
+        in_specs=[smem, smem] + [vmem] * (3 + 2 * back + ranks),
+        out_specs=[vmem] * (ranks + 5),
         scratch_shapes=[
+            pltpu.VMEM((tok, heads * width), jnp.bfloat16),
+            pltpu.VMEM((tok, heads * width), jnp.bfloat16),
             pltpu.VMEM((tok, heads, width), jnp.float32),
             pltpu.VMEM((span, width), jnp.bfloat16),
             pltpu.VMEM((span, 2 * width), jnp.bfloat16),
@@ -230,7 +254,81 @@
             transcendentals=tok * heads * span,
         ),
         name="attention",
-    )(doc_lengths, place, queries, grad_rows, own, near, far, *arrived)
+    )(doc_lengths, place, queries, own, near, *arrived, *far, *grad_parts)
+
+
+def pack_kernel(key_ref, value_ref, own_ref):
+    tok = key_ref.shape[0]
+    own_ref[0:tok, :] = key_ref[...]
+    own_ref[tok:, :] = value_ref[...]
+
+
+def pack(keys, values):
+    tok, width = keys.shape
+    vmem = pl.BlockSpec(memory_space=pltpu.VMEM)
+    return pl.pallas_call(
+        pack_kernel,
+        out_shape=jax.ShapeDtypeStruct((2 * tok, width), keys.dtype),
+        in_specs=[vmem, vmem],
+        out_specs=vmem,
+        name="pack",
+    )(keys, values)
+
+
+def split_kernel(place_ref, grad_ref, *part_refs):
+    size = part_refs[0].shape[1]
+    for k, ref in enumerate(part_refs):
+        at = pl.multiple_of((place_ref[3] ^ k) * size, size)
+        ref[...] = grad_ref[:, pl.ds(at, size)]
+
+
+def split(place, grad_attended, ranks):
+    rows, columns = grad_attended.shape
+    vmem = pl.BlockSpec(memory_space=pltpu.VMEM)
+    part = jax.ShapeDtypeStruct((rows, columns // ranks), grad_attended.dtype)
+    return pl.pallas_call(
+        split_kernel,
+        out_shape=[part] * ranks,
+        in_specs=[pl.BlockSpec(memory_space=pltpu.SMEM), vmem],
+        out_specs=[vmem] * ranks,
+        name="split",
+    )(place, grad_attended)
+
+
+def join_kernel(place_ref, *refs):
+    out_ref = refs[-1]
+    size = refs[0].shape[1]
+    for k, ref in enumerate(refs[:-1]):
+        at = pl.multiple_of((place_ref[3] ^ k) * size, size)
+        out_ref[:, pl.ds(at, size)] = ref[...]
+
+
+def join(place, parts):
+    rows, size = parts[0].shape
+    vmem = pl.BlockSpec(memory_space=pltpu.VMEM)
+    return pl.pallas_call(
+        join_kernel,
+        out_shape=jax.ShapeDtypeStruct((rows, size * len(parts)), parts[0].dtype),
+        in_specs=[pl.BlockSpec(memory_space=pltpu.SMEM)] + [vmem] * len(parts),
+        out_specs=vmem,
+        name="join",
+    )(place, *parts)
+
+
+def merge_kernel(mine_ref, other_ref, *block_refs):
+    for k, ref in enumerate(block_refs):
+        ref[...] = (mine_ref[k] + other_ref[k].astype(jnp.float32)).astype(ref.dtype)
+
+
+def merge(mine, other, dtypes):
+    vmem = pl.BlockSpec(memory_space=pltpu.VMEM)
+    return pl.pallas_call(
+        merge_kernel,
+        out_shape=[jax.ShapeDtypeStruct(mine.shape[1:], dtype) for dtype in dtypes],
+        in_specs=[vmem, vmem],
+        out_specs=[vmem] * len(dtypes),
+        name="merge",
+    )(mine, other)
 
 
 def finish_kernel(own_ref, *refs):
@@ -264,36 +362,48 @@
     return lax.ppermute(block, "ctx", pairs)
 
 
-def exchanged(block, count):
-    return lax.ppermute(block, "ctx", [(i, i ^ 1) for i in range(count)])
+def exchanged(block, axis, by):
+    return lax.ppermute(block, axis, [(i, i ^ by) for i in range(lax.axis_size(axis))])
 
 
 def body(queries, key_states, value_states, doc_lengths, grad_attended):
     tok, heads, width = queries.shape
     count = lax.axis_size("ctx")
+    ranks = lax.axis_size("head")
     ctx = lax.axis_index("ctx")
     reach = min((DOC_MOST + tok - 2) // tok, count - 1)
     back = min((reach + 1) // 2, count // 2 - 1)
-    own = jnp.concatenate(
-        [key_states.reshape(tok, width), value_states.reshape(tok, width)], axis=0
+    parity = ctx % 2
+    place = jnp.stack(
+        [(ctx - parity - 2 * back) * tok, 2 * back + parity, parity, lax.axis_index("head")]
+    ).astype(jnp.int32)
+    own = pack(key_states.reshape(tok, width), value_states.reshape(tok, width))
+    arrived = [shifted(own, 2 * k, count) for k in range(back, 0, -1)][::-1]
+    far = []
+    for block in arrived:
+        if far:
+            block, far[-1] = lax.optimization_barrier((block, far[-1]))
+        far.append(exchanged(block, "ctx", 1))
+    near = exchanged(own, "ctx", 1)
+    grad_parts = split(place, grad_attended, ranks)
+    grad_parts = [part if k == 0 else exchanged(part, "head", k) for k, part in enumerate(grad_parts)]
+    *out_parts, grad_queries, mine_first, mine_last, other_first, other_last = attend(
+        doc_lengths, place, queries, own, near, arrived, far, grad_parts
     )
-    near = exchanged(own, count)
-    arrived = [shifted(own, 2 * k, count) for k in range(1, back + 1)]
-    near, arrived, grad_attended = lax.optimization_barrier((near, arrived, grad_attended))
-    far = exchanged(jnp.concatenate(arrived, axis=0), count)
-    grad_rows = lax.all_to_all(grad_attended, "head", split_axis=1, concat_axis=0, tiled=True)
-    parity = ctx % 2
-    place = jnp.stack([(ctx - parity - 2 * back) * tok, 2 * back + parity, parity])
-    attended, grad_queries, d_mine, d_other = attend(
-        doc_lengths, place.astype(jnp.int32), queries, grad_rows, own, near, far, arrived
+    first = mine_first.shape[0]
+    out_parts = [part if k == 0 else exchanged(part, "head", k) for k, part in enumerate(out_parts)]
+    other_first = exchanged(other_first, "ctx", 1)
+    other_last = exchanged(other_last, "ctx", 1)
+    blocks = merge(mine_first, other_first, [jnp.bfloat16] * first)
+    arrived = [shifted(block, 2 * (pair - back), count) for pair, block in enumerate(blocks)]
+    *blocks, own_block = merge(
+        mine_last, other_last, [jnp.bfloat16] * (back - first) + [jnp.float32]
     )
-    d_near = exchanged(d_other, count)
-    attended = lax.all_to_all(attended, "head", split_axis=0, concat_axis=1, tiled=True)
-    total = d_mine + d_near.astype(jnp.float32)
-    arrived = [
-        shifted(total[back - k].astype(jnp.bfloat16), -2 * k, count) for k in range(back, 0, -1)
+    arrived += [
+        shifted(block, 2 * (first + k - back), count) for k, block in enumerate(blocks)
     ]
-    grad_keys, grad_values = finish(total[back], arrived)
+    grad_keys, grad_values = finish(own_block, arrived)
+    attended = join(place, out_parts)
     grad_keys = grad_keys.reshape(tok, 1, width)
     grad_values = grad_values.reshape(tok, 1, width)
     return attended, grad_queries, grad_keys, grad_values

time: 89.5 us -> 86.8 us (0.970)
  blocking collectives: 11.2 us -> 0 us
  Pallas kernels: 10.3 us -> 19.5 us
  waiting for transfers between devices: 37.4 us -> 29 us
  starting transfers between devices: 24.6 us -> 30.5 us
  local copies, waits for them, and re-layouts: 3.71 us -> 5.94 us
    ppermute x6, waiting for transfers between devices: 28.3 us -> 16.3 us  [shifted(): return lax.ppermute(block, 'ctx', pairs)]
    all_to_all x1 -> x0, blocking collectives: 11.2 us -> none  [body(): lax.all_to_all(attended, 'head', split_axis=0, concat_axis=1, tiled=True)]
    pallas_call x1 -> x6, Pallas kernels: 8.24 us -> 17.5 us  [the longest x1 8.31 us: attend(): pl.pallas_call(functools.partial(attention_kernel, back=back, ranks=ranks...]
    ppermute x3 -> x12, waiting for transfers between devices: 3.93 us -> 12.7 us  [exchanged(): lax.ppermute(block, axis, [(i, i ^ by) for i in range(lax.axis_size(axis))])]
    all_to_all x1 -> x0, waiting for transfers between devices: 5.22 us -> none  [body(): lax.all_to_all(grad_attended, 'head', split_axis=1, concat_axis=0, tiled=...]
    ppermute x6, starting transfers between devices: 14.6 us -> 19.4 us  [shifted(): return lax.ppermute(block, 'ctx', pairs)]
    ppermute x3 -> x12, starting transfers between devices: 6.37 us -> 11.1 us  [exchanged(): lax.ppermute(block, axis, [(i, i ^ by) for i in range(lax.axis_size(axis))])]
    unnamed x12 -> x32, local copies, waits for them, and re-layouts: 1.31 us -> 5.94 us
  transfers between devices with their start and end apart: 10 -> 18, of which waited for: 7 -> 5; matrix products, arithmetic and copies ran while one was open for 3% -> 1% of each run, Pallas kernels for 0% -> 9%
where the time goes in v2:
time: 86.8 us; the launch traced here: 86.5 us
  starting transfers between devices  30.5 us (35%)
  waiting for transfers between devices  29 us (33%)
  Pallas kernels  19.5 us (22%)
  local copies, waits for them, and re-layouts  5.94 us (7%)
    ppermute x6, starting transfers between devices, shifted(): return lax.ppermute(block, 'ctx', pairs)  19.4 us
    ppermute x6, waiting for transfers between devices, shifted(): return lax.ppermute(block, 'ctx', pairs)  16.3 us
    ppermute x12, waiting for transfers between devices, exchanged(): lax.ppermute(block, axis, [(i, i ^ by) for i in range(lax.axis_size(axis))])  12.7 us
    ppermute x12, starting transfers between devices, exchanged(): lax.ppermute(block, axis, [(i, i ^ by) for i in range(lax.axis_size(axis))])  11.1 us
    pallas_call x1, Pallas kernels, attend(): pl.pallas_call(functools.partial(attention_kernel, back=back, ranks=ranks...  8.31 us
    unnamed x32, local copies, waits for them, and re-layouts  5.94 us
    pallas_call x2, Pallas kernels, merge(): pl.pallas_call(merge_kernel, out_shape=[jax.ShapeDtypeStruct(mine.shape[1...  3.76 us
    pallas_call x1, Pallas kernels, finish(): pl.pallas_call(finish_kernel, out_shape=(shape, shape), in_specs=[vmem] *...  2.02 us
  transfers between devices with their start and end apart: 18, of which 5 were waited for; matrix products, arithmetic and copies ran while one was open for 1% of the time, Pallas kernels for 9%

profile of v2, /device:TPU:0, one launch (start us, length us, event | category | flops | bytes accessed | tf_op | source)
XLA Modules:
  0.0 86.5 jit_solution(13959964757712464639)
XLA Ops:
  0.6 0.0 copy-start.5
  0.6 1.6 %pack.1.own_ref = bf16[512,128]{1,0:T(8,128)(2,1)} custom-call(bf16[256,128]{1,0:T(8,128)(2,1)} %bitcast.8, bf16[256,128]{1,0:T(8,128)(2,1)} %bitcast.9), custom_call_target="tpu_custom_call" | custom-call | tf_op jit(solution)/shard_map/pack/pallas_call | solution.py:269
  2.2 4.9 %collective-permute-start.1 = (bf16[512,128]{1,0:T(8,128)(2,1)}, bf16[512,128]{1,0:T(8,128)(2,1)S(1)}, u32[]{:S(2)}, u32[]{:S(2)}) collective-permute-start(bf16[512,128]{1,0:T(8,128)(2,1)} %pack.1.own_ref), channel_id=1, source_target_pairs={{0,8},{4,12},{8,16},{12,20},{16,24},{20,28},{1,9},{5,13},{9,17},{1... | collective-permute-start | bytes 393224 | tf_op jit(solution)/shard_map/ppermute | solution.py:362
  7.2 4.5 %collective-permute-start.2 = (bf16[512,128]{1,0:T(8,128)(2,1)}, bf16[512,128]{1,0:T(8,128)(2,1)S(1)}, u32[]{:S(2)}, u32[]{:S(2)}) collective-permute-start(bf16[512,128]{1,0:T(8,128)(2,1)} %pack.1.own_ref), channel_id=1, source_target_pairs={{0,16},{4,20},{8,24},{12,28},{1,17},{5,21},{9,25},{13,29},{2,18},{... | collective-permute-start | bytes 393224 | tf_op jit(solution)/shard_map/ppermute | solution.py:362
  11.7 0.0 collective-permute-done.1.refs_0_
  11.7 1.6 %collective-permute-start.4 = (bf16[512,128]{1,0:T(8,128)(2,1)S(1)}, bf16[512,128]{1,0:T(8,128)(2,1)S(1)}, u32[]{:S(2)}, u32[]{:S(2)}) collective-permute-start(bf16[512,128]{1,0:T(8,128)(2,1)S(1)} %collective-permute-done.1.refs_0_), channel_id=1, source_target_pairs={{0,4},{4,0},{8,12},{12,8},{16,20},{20,16},{24,28},{28,24},{1,5},{5... | collective-permute-start | bytes 393224 | tf_op jit(solution)/shard_map/ppermute | solution.py:366
  13.3 6.2 %collective-permute-start.3 = (bf16[512,128]{1,0:T(8,128)(2,1)}, bf16[512,128]{1,0:T(8,128)(2,1)S(1)}, u32[]{:S(2)}, u32[]{:S(2)}) collective-permute-start(bf16[512,128]{1,0:T(8,128)(2,1)} %pack.1.own_ref), channel_id=1, source_target_pairs={{0,24},{4,28},{1,25},{5,29},{2,26},{6,30},{3,27},{7,31}} | collective-permute-start | bytes 393224 | tf_op jit(solution)/shard_map/ppermute | solution.py:362
  19.4 0.0 collective-permute-done.2.refs_1_
  19.5 0.0 collective-permute-done.4.refs_3_
  19.5 0.6 collective-permute-start.5
  20.0 1.5 %collective-permute-start = (bf16[512,128]{1,0:T(8,128)(2,1)}, bf16[512,128]{1,0:T(8,128)(2,1)S(1)}, u32[]{:S(2)}, u32[]{:S(2)}) collective-permute-start(bf16[512,128]{1,0:T(8,128)(2,1)} %pack.1.own_ref), channel_id=1, source_target_pairs={{0,4},{4,0},{8,12},{12,8},{16,20},{20,16},{24,28},{28,24},{1,5},{5... | collective-permute-start | bytes 393224 | tf_op jit(solution)/shard_map/ppermute | solution.py:366
  21.6 0.7 pad_add_fusion.place_ref
  22.2 1.9 %split.1 = (bf16[64,1024]{1,0:T(8,128)(2,1)}, bf16[64,1024]{1,0:T(8,128)(2,1)}, bf16[64,1024]{1,0:T(8,128)(2,1)}, bf16[64,1024]{1,0:T(8,128)(2,1)}) custom-call(s32[4]{0:T(128)} %pad_add_fusion.place_ref, bf16[64,4096]{1,0:T(8,128)(2,1)} %grad_ref.1), custom_call_target="tpu_custom_call" | custom-call | tf_op jit(solution)/shard_map/split/pallas_call | solution.py:289
  24.1 0.0 collective-permute-start.7
  24.1 1.5 %collective-permute-start.8 = (bf16[64,1024]{1,0:T(8,128)(2,1)}, bf16[64,1024]{1,0:T(8,128)(2,1)S(1)}, u32[]{:S(2)}, u32[]{:S(2)}) collective-permute-start(bf16[64,1024]{1,0:T(8,128)(2,1)} %get-tuple-element.33), channel_id=1, source_target_pairs={{0,2},{1,3},{2,0},{3,1},{4,6},{5,7},{6,4},{7,5},{8,10},{9,11},{10,... | collective-permute-start | bytes 393224 | tf_op jit(solution)/shard_map/ppermute | solution.py:366
  25.6 0.0 collective-permute-done.3.refs_2_
  25.6 0.4 collective-permute-start.9
  26.0 0.0 collective-permute-done.5.refs_4_
  26.0 0.5 collective-permute-start.6
  26.5 0.0 collective-permute-done.near_ref
  26.5 0.0 collective-permute-done.7.refs_7_
  26.5 4.1 %collective-permute-done.8.refs_8_ = bf16[64,1024]{1,0:T(8,128)(2,1)S(1)} collective-permute-done((bf16[64,1024]{1,0:T(8,128)(2,1)}, bf16[64,1024]{1,0:T(8,128)(2,1)S(1)}, u32[]{:S(2)}, u32[]{:S(2)}) %collective-permute-start.8) | collective-permute-done | bytes 131104 | tf_op jit(solution)/shard_map/ppermute | solution.py:366
  30.6 2.0 %collective-permute-done.9.refs_9_ = bf16[64,1024]{1,0:T(8,128)(2,1)S(1)} collective-permute-done((bf16[64,1024]{1,0:T(8,128)(2,1)}, bf16[64,1024]{1,0:T(8,128)(2,1)S(1)}, u32[]{:S(2)}, u32[]{:S(2)}) %collective-permute-start.9) | collective-permute-done | bytes 131104 | tf_op jit(solution)/shard_map/ppermute | solution.py:366
  32.7 0.0 collective-permute-done.6.refs_5_
  32.7 0.0 copy-done.5
  32.7 0.0 copy-done.2
  32.7 0.0 copy-done.4
  32.7 0.0 copy-done.7
  32.7 0.0 copy-start.6
  32.7 0.9 %copy-done.6 = bf16[64,1024]{1,0:T(8,128)(2,1)S(1)} copy-done((bf16[64,1024]{1,0:T(8,128)(2,1)S(1)}, bf16[64,1024]{1,0:T(8,128)(2,1)}, u32[]{:S(2)}) %copy-start.6) | copy-done | bytes 131096
  33.6 8.3 %attention.1 = (bf16[64,1024]{1,0:T(8,128)(2,1)S(1)}, bf16[64,1024]{1,0:T(8,128)(2,1)S(1)}, bf16[64,1024]{1,0:T(8,128)(2,1)S(1)}, bf16[64,1024]{1,0:T(8,128)(2,1...) custom-call(s32[8]{0:T(128)S(1)} %copy-done.7, ...), custom_call_target="tpu_custom_call" | custom-call | flops 7516192768 | bytes 4194304 | tf_op jit(solution)/shard_map/attention/pallas_call | solution.py:213
  41.9 0.8 copy-done
  42.7 0.8 copy-done.1
  43.5 0.6 copy-done.3
  44.2 3.1 %collective-permute-start.13 = (bf16[2,256,256]{2,1,0:T(8,128)(2,1)S(1)}, bf16[2,256,256]{2,1,0:T(8,128)(2,1)S(1)}, u32[]{:S(2)}, u32[]{:S(2)}) collective-permute-start(bf16[2,256,256]{2,1,0:T(8,128)(2,1)S(1)} %get-tuple-element.41), channel_id=1, source_target_pairs={{0,4},{4,0},{8,12},{12,8},{16,20},{20,16},{24,28},{28,24},{1,5},{5... | collective-permute-start | bytes 786440 | tf_op jit(solution)/shard_map/ppermute | solution.py:366
  47.3 0.0 collective-permute-start.14
  47.3 0.0 collective-permute-start.10
  47.3 1.5 %collective-permute-start.11 = (bf16[64,1024]{1,0:T(8,128)(2,1)S(1)}, bf16[64,1024]{1,0:T(8,128)(2,1)S(1)}, u32[]{:S(2)}, u32[]{:S(2)}) collective-permute-start(bf16[64,1024]{1,0:T(8,128)(2,1)S(1)} %get-tuple-element.37), channel_id=1, source_target_pairs={{0,2},{1,3},{2,0},{3,1},{4,6},{5,7},{6,4},{7,5},{8,10},{9,11},{10,... | collective-permute-start | bytes 393224 | tf_op jit(solution)/shard_map/ppermute | solution.py:366
  48.9 0.3 collective-permute-start.12
  49.2 5.2 %collective-permute-done.13.other_ref = bf16[2,256,256]{2,1,0:T(8,128)(2,1)S(1)} collective-permute-done((bf16[2,256,256]{2,1,0:T(8,128)(2,1)S(1)}, bf16[2,256,256]{2,1,0:T(8,128)(2,1)S(1)}, u32[]{:S(2)}, u32[]{:S(2)}) %collective-permute-start.13) | collective-permute-done | bytes 262176 | tf_op jit(solution)/shard_map/ppermute | solution.py:366
  54.4 0.7 copy-done.9
  55.1 1.9 %merge.2 = (bf16[256,256]{1,0:T(8,128)(2,1)}, f32[256,256]{1,0:T(8,128)}) custom-call(f32[2,256,256]{2,1,0:T(8,128)} %copy-done.1, bf16[2,256,256]{2,1,0:T(8,128)(2,1)} %copy-done.9), custom_call_target="tpu_custom_call" | custom-call | tf_op jit(solution)/shard_map/merge/pallas_call | solution.py:325
  57.0 1.3 %collective-permute-start.17 = (bf16[256,256]{1,0:T(8,128)(2,1)}, bf16[256,256]{1,0:T(8,128)(2,1)S(1)}, u32[]{:S(2)}, u32[]{:S(2)}) collective-permute-start(bf16[256,256]{1,0:T(8,128)(2,1)} %get-tuple-element.47), channel_id=1, source_target_pairs={{8,0},{12,4},{16,8},{20,12},{24,16},{28,20},{9,1},{13,5},{17,9},{2... | collective-permute-start | bytes 393224 | tf_op jit(solution)/shard_map/ppermute | solution.py:362
  58.3 1.3 %collective-permute-done.14.other_ref = bf16[2,256,256]{2,1,0:T(8,128)(2,1)S(1)} collective-permute-done((bf16[2,256,256]{2,1,0:T(8,128)(2,1)S(1)}, bf16[2,256,256]{2,1,0:T(8,128)(2,1)S(1)}, u32[]{:S(2)}, u32[]{:S(2)}) %collective-permute-start.14) | collective-permute-done | bytes 262176 | tf_op jit(solution)/shard_map/ppermute | solution.py:366
  59.6 0.7 copy-done.8
  60.3 1.8 %merge.3 = (bf16[256,256]{1,0:T(8,128)(2,1)}, bf16[256,256]{1,0:T(8,128)(2,1)}) custom-call(f32[2,256,256]{2,1,0:T(8,128)} %copy-done, bf16[2,256,256]{2,1,0:T(8,128)(2,1)} %copy-done.8), custom_call_target="tpu_custom_call" | custom-call | tf_op jit(solution)/shard_map/merge/pallas_call | solution.py:325
  62.1 1.3 %collective-permute-start.15 = (bf16[256,256]{1,0:T(8,128)(2,1)}, bf16[256,256]{1,0:T(8,128)(2,1)S(1)}, u32[]{:S(2)}, u32[]{:S(2)}) collective-permute-start(bf16[256,256]{1,0:T(8,128)(2,1)} %get-tuple-element.45), channel_id=1, source_target_pairs={{24,0},{28,4},{25,1},{29,5},{26,2},{30,6},{27,3},{31,7}} | collective-permute-start | bytes 393224 | tf_op jit(solution)/shard_map/ppermute | solution.py:362
  63.4 0.0 collective-permute-done.10.refs_1_
  63.4 0.0 copy-start.13
  63.5 1.3 %collective-permute-start.16 = (bf16[256,256]{1,0:T(8,128)(2,1)}, bf16[256,256]{1,0:T(8,128)(2,1)S(1)}, u32[]{:S(2)}, u32[]{:S(2)}) collective-permute-start(bf16[256,256]{1,0:T(8,128)(2,1)} %get-tuple-element.46), channel_id=1, source_target_pairs={{16,0},{20,4},{24,8},{28,12},{17,1},{21,5},{25,9},{29,13},{18,2},{... | collective-permute-start | bytes 393224 | tf_op jit(solution)/shard_map/ppermute | solution.py:362
  64.8 0.0 collective-permute-done.11.refs_2_
  64.8 0.0 copy-start.14
  64.8 0.0 collective-permute-done.12.refs_3_
  64.8 0.0 copy-start.15
  64.8 0.0 copy-done.13
  64.8 0.6 copy-done.14
  65.4 0.1 copy-done.15
  65.5 1.9 %join.1 = bf16[64,4096]{1,0:T(8,128)(2,1)} custom-call(s32[4]{0:T(128)} %pad_add_fusion.place_ref, bf16[64,1024]{1,0:T(8,128)(2,1)} %copy-done.3, bf16[64,1024]{1,0:T(8,128)(2,1)} %copy-done.13, bf16[64,1024]{1,0:T(8,128)(2,1)} %copy-done.14, bf16[64,1024]{1,0:T(8,128)(2,1)} %copy-done.15), custom_call_target="tpu_custom_call" | custom-call | tf_op jit(solution)/shard_map/join/pallas_call | solution.py:309
  67.4 0.0 collective-permute-done.17.refs_2_
  67.4 16.3 %collective-permute-done.15.refs_0_ = bf16[256,256]{1,0:T(8,128)(2,1)S(1)} collective-permute-done((bf16[256,256]{1,0:T(8,128)(2,1)}, bf16[256,256]{1,0:T(8,128)(2,1)S(1)}, u32[]{:S(2)}, u32[]{:S(2)}) %collective-permute-start.15) | collective-permute-done | bytes 131104 | tf_op jit(solution)/shard_map/ppermute | solution.py:362
  83.7 0.0 collective-permute-done.16.refs_1_
  83.7 0.6 copy-done.11
  84.4 0.1 copy-done.12
  84.4 2.0 %finish.1 = (bf16[256,128]{1,0:T(8,128)(2,1)}, bf16[256,128]{1,0:T(8,128)(2,1)}) custom-call(f32[256,256]{1,0:T(8,128)} %get-tuple-element.42.own_ref, bf16[256,256]{1,0:T(8,128)(2,1)} %copy-done.11, bf16[256,256]{1,0:T(8,128)(2,1)} %copy-done.12, bf16[256,256]{1,0:T(8,128)(2,1)} %copy-done.10), custom_call_target="tpu_custom_call" | custom-call | tf_op jit(solution)/shard_map/finish/pallas_call | solution.py:351
  (12 shorter events, 0.0 us)
Async XLA Ops:
  0.6 32.0 %copy-start.5 = (bf16[256,8,128]{2,1,0:T(8,128)(2,1)S(1)}, bf16[256,8,128]{2,1,0:T(8,128)(2,1)}, u32[]{:S(2)}) copy-start(bf16[256,8,128]{2,1,0:T(8,128)(2,1)} %q_ref.1) | copy-start | bytes 1572868
  2.2 9.4 %collective-permute-start.1 = (bf16[512,128]{1,0:T(8,128)(2,1)}, bf16[512,128]{1,0:T(8,128)(2,1)S(1)}, u32[]{:S(2)}, u32[]{:S(2)}) collective-permute-start(bf16[512,128]{1,0:T(8,128)(2,1)} %pack.1.own_ref), channel_id=1, source_target_pairs={{0,8},{4,12},{8,16},{12,20},{16,24},{20,28},{1,9},{5,13},{9,17},{1... | collective-permute-start | bytes 393224 | tf_op jit(solution)/shard_map/ppermute | solution.py:362
  7.2 12.3 %collective-permute-start.2 = (bf16[512,128]{1,0:T(8,128)(2,1)}, bf16[512,128]{1,0:T(8,128)(2,1)S(1)}, u32[]{:S(2)}, u32[]{:S(2)}) collective-permute-start(bf16[512,128]{1,0:T(8,128)(2,1)} %pack.1.own_ref), channel_id=1, source_target_pairs={{0,16},{4,20},{8,24},{12,28},{1,17},{5,21},{9,25},{13,29},{2,18},{... | collective-permute-start | bytes 393224 | tf_op jit(solution)/shard_map/ppermute | solution.py:362
  11.7 7.8 %collective-permute-start.4 = (bf16[512,128]{1,0:T(8,128)(2,1)S(1)}, bf16[512,128]{1,0:T(8,128)(2,1)S(1)}, u32[]{:S(2)}, u32[]{:S(2)}) collective-permute-start(bf16[512,128]{1,0:T(8,128)(2,1)S(1)} %collective-permute-done.1.refs_0_), channel_id=1, source_target_pairs={{0,4},{4,0},{8,12},{12,8},{16,20},{20,16},{24,28},{28,24},{1,5},{5... | collective-permute-start | bytes 393224 | tf_op jit(solution)/shard_map/ppermute | solution.py:366
  13.3 12.4 %collective-permute-start.3 = (bf16[512,128]{1,0:T(8,128)(2,1)}, bf16[512,128]{1,0:T(8,128)(2,1)S(1)}, u32[]{:S(2)}, u32[]{:S(2)}) collective-permute-start(bf16[512,128]{1,0:T(8,128)(2,1)} %pack.1.own_ref), channel_id=1, source_target_pairs={{0,24},{4,28},{1,25},{5,29},{2,26},{6,30},{3,27},{7,31}} | collective-permute-start | bytes 393224 | tf_op jit(solution)/shard_map/ppermute | solution.py:362
  19.5 6.5 %collective-permute-start.5 = (bf16[512,128]{1,0:T(8,128)(2,1)S(1)}, bf16[512,128]{1,0:T(8,128)(2,1)S(1)}, u32[]{:S(2)}, u32[]{:S(2)}) collective-permute-start(bf16[512,128]{1,0:T(8,128)(2,1)S(1)} %collective-permute-done.2.refs_1_), channel_id=1, source_target_pairs={{0,4},{4,0},{8,12},{12,8},{16,20},{20,16},{24,28},{28,24},{1,5},{5... | collective-permute-start | bytes 393224 | tf_op jit(solution)/shard_map/ppermute | solution.py:366
  20.0 6.5 %collective-permute-start = (bf16[512,128]{1,0:T(8,128)(2,1)}, bf16[512,128]{1,0:T(8,128)(2,1)S(1)}, u32[]{:S(2)}, u32[]{:S(2)}) collective-permute-start(bf16[512,128]{1,0:T(8,128)(2,1)} %pack.1.own_ref), channel_id=1, source_target_pairs={{0,4},{4,0},{8,12},{12,8},{16,20},{20,16},{24,28},{28,24},{1,5},{5... | collective-permute-start | bytes 393224 | tf_op jit(solution)/shard_map/ppermute | solution.py:366
  22.2 10.5 %copy-start.2 = (bf16[512,128]{1,0:T(8,128)(2,1)S(1)}, bf16[512,128]{1,0:T(8,128)(2,1)}, u32[]{:S(2)}) copy-start(bf16[512,128]{1,0:T(8,128)(2,1)} %pack.1.own_ref) | copy-start | bytes 393220
  24.1 2.4 %collective-permute-start.7 = (bf16[64,1024]{1,0:T(8,128)(2,1)}, bf16[64,1024]{1,0:T(8,128)(2,1)S(1)}, u32[]{:S(2)}, u32[]{:S(2)}) collective-permute-start(bf16[64,1024]{1,0:T(8,128)(2,1)} %get-tuple-element.32), channel_id=1, source_target_pairs={{0,1},{1,0},{2,3},{3,2},{4,5},{5,4},{6,7},{7,6},{8,9},{9,8},{10,11... | collective-permute-start | bytes 393224 | tf_op jit(solution)/shard_map/ppermute | solution.py:366
  24.1 6.5 %collective-permute-start.8 = (bf16[64,1024]{1,0:T(8,128)(2,1)}, bf16[64,1024]{1,0:T(8,128)(2,1)S(1)}, u32[]{:S(2)}, u32[]{:S(2)}) collective-permute-start(bf16[64,1024]{1,0:T(8,128)(2,1)} %get-tuple-element.33), channel_id=1, source_target_pairs={{0,2},{1,3},{2,0},{3,1},{4,6},{5,7},{6,4},{7,5},{8,10},{9,11},{10,... | collective-permute-start | bytes 393224 | tf_op jit(solution)/shard_map/ppermute | solution.py:366
  25.6 7.1 %copy-start.4 = (s32[4]{0:T(128)S(1)}, s32[4]{0:T(128)}, u32[]{:S(2)}) copy-start(s32[4]{0:T(128)} %pad_add_fusion.place_ref) | copy-start | bytes 52
  25.6 7.1 %copy-start.7 = (s32[8]{0:T(128)S(1)}, s32[8]{0:T(128)}, u32[]{:S(2)}) copy-start(s32[8]{0:T(128)} %doc_ref.1) | copy-start | bytes 100
  25.6 7.0 %collective-permute-start.9 = (bf16[64,1024]{1,0:T(8,128)(2,1)}, bf16[64,1024]{1,0:T(8,128)(2,1)S(1)}, u32[]{:S(2)}, u32[]{:S(2)}) collective-permute-start(bf16[64,1024]{1,0:T(8,128)(2,1)} %get-tuple-element.34), channel_id=1, source_target_pairs={{0,3},{1,2},{2,1},{3,0},{4,7},{5,6},{6,5},{7,4},{8,11},{9,10},{10,... | collective-permute-start | bytes 393224 | tf_op jit(solution)/shard_map/ppermute | solution.py:366
  26.0 6.7 %collective-permute-start.6 = (bf16[512,128]{1,0:T(8,128)(2,1)S(1)}, bf16[512,128]{1,0:T(8,128)(2,1)S(1)}, u32[]{:S(2)}, u32[]{:S(2)}) collective-permute-start(bf16[512,128]{1,0:T(8,128)(2,1)S(1)} %collective-permute-done.3.refs_2_), channel_id=1, source_target_pairs={{0,4},{4,0},{8,12},{12,8},{16,20},{20,16},{24,28},{28,24},{1,5},{5... | collective-permute-start | bytes 393224 | tf_op jit(solution)/shard_map/ppermute | solution.py:366
  32.7 0.9 %copy-start.6 = (bf16[64,1024]{1,0:T(8,128)(2,1)S(1)}, bf16[64,1024]{1,0:T(8,128)(2,1)}, u32[]{:S(2)}) copy-start(bf16[64,1024]{1,0:T(8,128)(2,1)} %get-tuple-element.31.refs_6_) | copy-start | bytes 393220
  41.9 0.8 copy-start
  42.7 0.8 copy-start.1
  43.5 0.6 copy-start.3
  44.2 10.2 %collective-permute-start.13 = (bf16[2,256,256]{2,1,0:T(8,128)(2,1)S(1)}, bf16[2,256,256]{2,1,0:T(8,128)(2,1)S(1)}, u32[]{:S(2)}, u32[]{:S(2)}) collective-permute-start(bf16[2,256,256]{2,1,0:T(8,128)(2,1)S(1)} %get-tuple-element.41), channel_id=1, source_target_pairs={{0,4},{4,0},{8,12},{12,8},{16,20},{20,16},{24,28},{28,24},{1,5},{5... | collective-permute-start | bytes 786440 | tf_op jit(solution)/shard_map/ppermute | solution.py:366
  47.3 12.3 %collective-permute-start.14 = (bf16[2,256,256]{2,1,0:T(8,128)(2,1)S(1)}, bf16[2,256,256]{2,1,0:T(8,128)(2,1)S(1)}, u32[]{:S(2)}, u32[]{:S(2)}) collective-permute-start(bf16[2,256,256]{2,1,0:T(8,128)(2,1)S(1)} %get-tuple-element.44), channel_id=1, source_target_pairs={{0,4},{4,0},{8,12},{12,8},{16,20},{20,16},{24,28},{28,24},{1,5},{5... | collective-permute-start | bytes 786440 | tf_op jit(solution)/shard_map/ppermute | solution.py:366
  47.3 16.1 %collective-permute-start.10 = (bf16[64,1024]{1,0:T(8,128)(2,1)S(1)}, bf16[64,1024]{1,0:T(8,128)(2,1)S(1)}, u32[]{:S(2)}, u32[]{:S(2)}) collective-permute-start(bf16[64,1024]{1,0:T(8,128)(2,1)S(1)} %get-tuple-element.36), channel_id=1, source_target_pairs={{0,1},{1,0},{2,3},{3,2},{4,5},{5,4},{6,7},{7,6},{8,9},{9,8},{10,11... | collective-permute-start | bytes 393224 | tf_op jit(solution)/shard_map/ppermute | solution.py:366
  47.3 17.4 %collective-permute-start.11 = (bf16[64,1024]{1,0:T(8,128)(2,1)S(1)}, bf16[64,1024]{1,0:T(8,128)(2,1)S(1)}, u32[]{:S(2)}, u32[]{:S(2)}) collective-permute-start(bf16[64,1024]{1,0:T(8,128)(2,1)S(1)} %get-tuple-element.37), channel_id=1, source_target_pairs={{0,2},{1,3},{2,0},{3,1},{4,6},{5,7},{6,4},{7,5},{8,10},{9,11},{10,... | collective-permute-start | bytes 393224 | tf_op jit(solution)/shard_map/ppermute | solution.py:366
  48.9 15.9 %collective-permute-start.12 = (bf16[64,1024]{1,0:T(8,128)(2,1)S(1)}, bf16[64,1024]{1,0:T(8,128)(2,1)S(1)}, u32[]{:S(2)}, u32[]{:S(2)}) collective-permute-start(bf16[64,1024]{1,0:T(8,128)(2,1)S(1)} %get-tuple-element.38), channel_id=1, source_target_pairs={{0,3},{1,2},{2,1},{3,0},{4,7},{5,6},{6,5},{7,4},{8,11},{9,10},{10,... | collective-permute-start | bytes 393224 | tf_op jit(solution)/shard_map/ppermute | solution.py:366
  54.4 0.7 copy-start.9
  57.0 10.4 %collective-permute-start.17 = (bf16[256,256]{1,0:T(8,128)(2,1)}, bf16[256,256]{1,0:T(8,128)(2,1)S(1)}, u32[]{:S(2)}, u32[]{:S(2)}) collective-permute-start(bf16[256,256]{1,0:T(8,128)(2,1)} %get-tuple-element.47), channel_id=1, source_target_pairs={{8,0},{12,4},{16,8},{20,12},{24,16},{28,20},{9,1},{13,5},{17,9},{2... | collective-permute-start | bytes 393224 | tf_op jit(solution)/shard_map/ppermute | solution.py:362
  59.6 0.7 copy-start.8
  62.1 21.6 %collective-permute-start.15 = (bf16[256,256]{1,0:T(8,128)(2,1)}, bf16[256,256]{1,0:T(8,128)(2,1)S(1)}, u32[]{:S(2)}, u32[]{:S(2)}) collective-permute-start(bf16[256,256]{1,0:T(8,128)(2,1)} %get-tuple-element.45), channel_id=1, source_target_pairs={{24,0},{28,4},{25,1},{29,5},{26,2},{30,6},{27,3},{31,7}} | collective-permute-start | bytes 393224 | tf_op jit(solution)/shard_map/ppermute | solution.py:362
  63.4 1.4 %copy-start.13 = (bf16[64,1024]{1,0:T(8,128)(2,1)}, bf16[64,1024]{1,0:T(8,128)(2,1)S(1)}, u32[]{:S(2)}) copy-start(bf16[64,1024]{1,0:T(8,128)(2,1)S(1)} %collective-permute-done.10.refs_1_) | copy-start | bytes 393220
  63.5 20.3 %collective-permute-start.16 = (bf16[256,256]{1,0:T(8,128)(2,1)}, bf16[256,256]{1,0:T(8,128)(2,1)S(1)}, u32[]{:S(2)}, u32[]{:S(2)}) collective-permute-start(bf16[256,256]{1,0:T(8,128)(2,1)} %get-tuple-element.46), channel_id=1, source_target_pairs={{16,0},{20,4},{24,8},{28,12},{17,1},{21,5},{25,9},{29,13},{18,2},{... | collective-permute-start | bytes 393224 | tf_op jit(solution)/shard_map/ppermute | solution.py:362
  64.8 0.7 copy-start.14
  64.8 0.7 copy-start.15
  67.4 16.3 %copy-start.10 = (bf16[256,256]{1,0:T(8,128)(2,1)}, bf16[256,256]{1,0:T(8,128)(2,1)S(1)}, u32[]{:S(2)}) copy-start(bf16[256,256]{1,0:T(8,128)(2,1)S(1)} %collective-permute-done.17.refs_2_) | copy-start | bytes 393220
  83.7 0.6 copy-start.11
  83.7 0.7 copy-start.12

commit v3 on v2

--- a/solution.py
+++ b/solution.py
@@ -13,6 +13,7 @@
 TILE = 256
 CHUNK = 128
 LOG2_E = 1.4426950408889634
+SMALL_VMEM = 8 * 1024 * 1024
 
 
 def dot(a, b):
@@ -34,7 +35,6 @@
 
 def attention_kernel(
     doc_ref,
-    place_ref,
     q_ref,
     own_ref,
     near_ref,
@@ -73,10 +73,11 @@
     tok = q_ref.shape[0]
     part_rows = tok // ranks
     docs = doc_ref.shape[0]
-    base = place_ref[0]
-    own = place_ref[1]
-    parity = place_ref[2]
-    rank = place_ref[3]
+    ctx = lax.axis_index("ctx")
+    rank = lax.axis_index("head")
+    parity = lax.rem(ctx, 2)
+    base = (ctx - parity - 2 * back) * tok
+    own = 2 * back + parity
     small = unit(width)
     ones = jnp.ones((width, width), jnp.bfloat16)
 
@@ -199,7 +200,7 @@
         ref[to, width:, :] = d_blocks[other, width:, :].astype(jnp.bfloat16)
 
 
-def attend(doc_lengths, place, queries, own, near, arrived, far, grad_parts):
+def attend(doc_lengths, queries, own, near, arrived, far, grad_parts):
     tok, heads, width = queries.shape
     back = len(arrived)
     ranks = len(grad_parts)
@@ -228,7 +229,7 @@
             for dtype in (jnp.float32, jnp.bfloat16)
             for size in (first, back + 1 - first)
         ],
-        in_specs=[smem, smem] + [vmem] * (3 + 2 * back + ranks),
+        in_specs=[smem] + [vmem] * (3 + 2 * back + ranks),
         out_specs=[vmem] * (ranks + 5),
         scratch_shapes=[
             pltpu.VMEM((tok, heads * width), jnp.bfloat16),
@@ -254,7 +255,7 @@
             transcendentals=tok * heads * span,
         ),
         name="attention",
-    )(doc_lengths, place, queries, own, near, *arrived, *far, *grad_parts)
+    )(doc_lengths, queries, own, near, *arrived, *far, *grad_parts)
 
 
 def pack_kernel(key_ref, value_ref, own_ref):
@@ -271,48 +272,51 @@
         out_shape=jax.ShapeDtypeStruct((2 * tok, width), keys.dtype),
         in_specs=[vmem, vmem],
         out_specs=vmem,
+        compiler_params=pltpu.CompilerParams(vmem_limit_bytes=SMALL_VMEM),
         name="pack",
     )(keys, values)
 
 
-def split_kernel(place_ref, grad_ref, *part_refs):
+def split_kernel(grad_ref, *part_refs):
     size = part_refs[0].shape[1]
     for k, ref in enumerate(part_refs):
-        at = pl.multiple_of((place_ref[3] ^ k) * size, size)
+        at = pl.multiple_of((lax.axis_index("head") ^ k) * size, size)
         ref[...] = grad_ref[:, pl.ds(at, size)]
 
 
-def split(place, grad_attended, ranks):
+def split(grad_attended, ranks):
     rows, columns = grad_attended.shape
     vmem = pl.BlockSpec(memory_space=pltpu.VMEM)
     part = jax.ShapeDtypeStruct((rows, columns // ranks), grad_attended.dtype)
     return pl.pallas_call(
         split_kernel,
         out_shape=[part] * ranks,
-        in_specs=[pl.BlockSpec(memory_space=pltpu.SMEM), vmem],
+        in_specs=[vmem],
         out_specs=[vmem] * ranks,
+        compiler_params=pltpu.CompilerParams(vmem_limit_bytes=SMALL_VMEM),
         name="split",
-    )(place, grad_attended)
-
-
-def join_kernel(place_ref, *refs):
+    )(grad_attended)
+
+
+def join_kernel(*refs):
     out_ref = refs[-1]
     size = refs[0].shape[1]
     for k, ref in enumerate(refs[:-1]):
-        at = pl.multiple_of((place_ref[3] ^ k) * size, size)
+        at = pl.multiple_of((lax.axis_index("head") ^ k) * size, size)
         out_ref[:, pl.ds(at, size)] = ref[...]
 
 
-def join(place, parts):
+def join(parts):
     rows, size = parts[0].shape
     vmem = pl.BlockSpec(memory_space=pltpu.VMEM)
     return pl.pallas_call(
         join_kernel,
         out_shape=jax.ShapeDtypeStruct((rows, size * len(parts)), parts[0].dtype),
-        in_specs=[pl.BlockSpec(memory_space=pltpu.SMEM)] + [vmem] * len(parts),
+        in_specs=[vmem] * len(parts),
         out_specs=vmem,
+        compiler_params=pltpu.CompilerParams(vmem_limit_bytes=SMALL_VMEM),
         name="join",
-    )(place, *parts)
+    )(*parts)
 
 
 def merge_kernel(mine_ref, other_ref, *block_refs):
@@ -327,6 +331,7 @@
         out_shape=[jax.ShapeDtypeStruct(mine.shape[1:], dtype) for dtype in dtypes],
         in_specs=[vmem, vmem],
         out_specs=[vmem] * len(dtypes),
+        compiler_params=pltpu.CompilerParams(vmem_limit_bytes=SMALL_VMEM),
         name="merge",
     )(mine, other)
 
@@ -353,6 +358,7 @@
         out_shape=(shape, shape),
         in_specs=[vmem] * (1 + len(arrived)),
         out_specs=(vmem, vmem),
+        compiler_params=pltpu.CompilerParams(vmem_limit_bytes=SMALL_VMEM),
         name="finish",
     )(own_part, *arrived)
 
@@ -370,25 +376,22 @@
     tok, heads, width = queries.shape
     count = lax.axis_size("ctx")
     ranks = lax.axis_size("head")
-    ctx = lax.axis_index("ctx")
     reach = min((DOC_MOST + tok - 2) // tok, count - 1)
     back = min((reach + 1) // 2, count // 2 - 1)
-    parity = ctx % 2
-    place = jnp.stack(
-        [(ctx - parity - 2 * back) * tok, 2 * back + parity, parity, lax.axis_index("head")]
-    ).astype(jnp.int32)
     own = pack(key_states.reshape(tok, width), value_states.reshape(tok, width))
-    arrived = [shifted(own, 2 * k, count) for k in range(back, 0, -1)][::-1]
+    arrived = [shifted(own, 2 * k, count) for k in range(1, back + 1)]
+    near = exchanged(own, "ctx", 1)
+    grad_parts = split(grad_attended, ranks)
+    grad_parts = [part if k == 0 else exchanged(part, "head", k) for k, part in enumerate(grad_parts)]
     far = []
-    for block in arrived:
+    for k, block in enumerate(arrived):
+        if k + 1 < ranks:
+            block, grad_parts[k + 1] = lax.optimization_barrier((block, grad_parts[k + 1]))
         if far:
             block, far[-1] = lax.optimization_barrier((block, far[-1]))
         far.append(exchanged(block, "ctx", 1))
-    near = exchanged(own, "ctx", 1)
-    grad_parts = split(place, grad_attended, ranks)
-    grad_parts = [part if k == 0 else exchanged(part, "head", k) for k, part in enumerate(grad_parts)]
     *out_parts, grad_queries, mine_first, mine_last, other_first, other_last = attend(
-        doc_lengths, place, queries, own, near, arrived, far, grad_parts
+        doc_lengths, queries, own, near, arrived, far, grad_parts
     )
     first = mine_first.shape[0]
     out_parts = [part if k == 0 else exchanged(part, "head", k) for k, part in enumerate(out_parts)]
@@ -396,6 +399,7 @@
     other_last = exchanged(other_last, "ctx", 1)
     blocks = merge(mine_first, other_first, [jnp.bfloat16] * first)
     arrived = [shifted(block, 2 * (pair - back), count) for pair, block in enumerate(blocks)]
+    other_last, arrived[0] = lax.optimization_barrier((other_last, arrived[0]))
     *blocks, own_block = merge(
         mine_last, other_last, [jnp.bfloat16] * (back - first) + [jnp.float32]
     )
@@ -403,7 +407,7 @@
         shifted(block, 2 * (first + k - back), count) for k, block in enumerate(blocks)
     ]
     grad_keys, grad_values = finish(own_block, arrived)
-    attended = join(place, out_parts)
+    attended = join(out_parts)
     grad_keys = grad_keys.reshape(tok, 1, width)
     grad_values = grad_values.reshape(tok, 1, width)
     return attended, grad_queries, grad_keys, grad_values

time: 86.8 us -> 81.8 us (0.942)
  waiting for transfers between devices: 29 us -> 40.9 us
  Pallas kernels: 19.5 us -> 10.2 us
  starting transfers between devices: 30.5 us -> 26.8 us
  local copies, waits for them, and re-layouts: 5.94 us -> 2.72 us
    ppermute x6, waiting for transfers between devices: 16.3 us -> 23.5 us  [shifted(): return lax.ppermute(block, 'ctx', pairs)]
    ppermute x12, waiting for transfers between devices: 12.7 us -> 17.4 us  [exchanged(): lax.ppermute(block, axis, [(i, i ^ by) for i in range(lax.axis_size(axis))])]
    ppermute x6, starting transfers between devices: 19.4 us -> 15.2 us  [shifted(): return lax.ppermute(block, 'ctx', pairs)]
    pallas_call x2, Pallas kernels: 3.76 us -> 0.11 us  [merge(): pl.pallas_call(merge_kernel, out_shape=[jax.ShapeDtypeStruct(mine.shape[1...]
    unnamed x32 -> x10, local copies, waits for them, and re-layouts: 5.94 us -> 2.72 us
    pallas_call x1, Pallas kernels: 1.91 us -> 0.03 us  [split(): pl.pallas_call(split_kernel, out_shape=[part] * ranks, in_specs=[vmem], o...]
    pallas_call x1, Pallas kernels: 1.59 us -> 0.01 us  [pack(): pl.pallas_call(pack_kernel, out_shape=jax.ShapeDtypeStruct((2 * tok, widt...]
    pallas_call x1, Pallas kernels: 2.02 us -> 0.91 us  [finish(): pl.pallas_call(finish_kernel, out_shape=(shape, shape), in_specs=[vmem] *...]
  transfers between devices with their start and end apart: 18 -> 18, of which waited for: 5 -> 9; matrix products, arithmetic and copies ran while one was open for 1% -> 0% of each run, Pallas kernels for 9% -> 1%
where the time goes in v3:
time: 81.8 us; the launch traced here: 81.5 us
  waiting for transfers between devices  40.9 us (50%)
  starting transfers between devices  26.8 us (33%)
  Pallas kernels  10.2 us (12%)
  local copies, waits for them, and re-layouts  2.72 us (3%)
    ppermute x6, waiting for transfers between devices, shifted(): return lax.ppermute(block, 'ctx', pairs)  23.5 us
    ppermute x12, waiting for transfers between devices, exchanged(): lax.ppermute(block, axis, [(i, i ^ by) for i in range(lax.axis_size(axis))])  17.4 us
    ppermute x6, starting transfers between devices, shifted(): return lax.ppermute(block, 'ctx', pairs)  15.2 us
    ppermute x12, starting transfers between devices, exchanged(): lax.ppermute(block, axis, [(i, i ^ by) for i in range(lax.axis_size(axis))])  11.6 us
    pallas_call x1, Pallas kernels, attend(): pl.pallas_call(functools.partial(attention_kernel, back=back, ranks=ranks...  8.3 us
    unnamed x10, local copies, waits for them, and re-layouts  2.72 us
  transfers between devices with their start and end apart: 18, of which 9 were waited for; matrix products, arithmetic and copies ran while one was open for 0% of the time, Pallas kernels for 1%

profile of v3, /device:TPU:0, one launch (start us, length us, event | category | flops | bytes accessed | tf_op | source)
XLA Modules:
  0.0 81.5 jit_solution(7209912703569554987)
XLA Ops:
  0.6 0.0 copy-start.1
  0.6 0.8 %copy-done.1 = bf16[256,1,128]{2,0,1:T(8,128)(2,1)S(1)} copy-done((bf16[256,1,128]{2,0,1:T(8,128)(2,1)S(1)}, bf16[256,1,128]{2,0,1:T(8,128)(2,1)}, u32[]{:S(2)}) %copy-start.1) | copy-done | bytes 65560
  1.5 0.0 copy-start.2
  1.5 0.8 %copy-done.2 = bf16[256,1,128]{2,0,1:T(8,128)(2,1)S(1)} copy-done((bf16[256,1,128]{2,0,1:T(8,128)(2,1)S(1)}, bf16[256,1,128]{2,0,1:T(8,128)(2,1)}, u32[]{:S(2)}) %copy-start.2) | copy-done | bytes 65560
  2.3 4.9 %collective-permute-start.1 = (bf16[512,128]{1,0:T(8,128)(2,1)S(1)}, bf16[512,128]{1,0:T(8,128)(2,1)S(1)}, u32[]{:S(2)}, u32[]{:S(2)}) collective-permute-start(bf16[512,128]{1,0:T(8,128)(2,1)S(1)} %pack.1.own_ref), channel_id=1, source_target_pairs={{0,8},{4,12},{8,16},{12,20},{16,24},{20,28},{1,9},{5,13},{9,17},{1... | collective-permute-start | bytes 393224 | tf_op jit(solution)/shard_map/ppermute | solution.py:368
  7.3 0.0 copy-start
  7.3 1.0 %copy-done = bf16[64,4096]{1,0:T(8,128)(2,1)S(1)} copy-done((bf16[64,4096]{1,0:T(8,128)(2,1)S(1)}, bf16[64,4096]{1,0:T(8,128)(2,1)}, u32[]{:S(2)}) %copy-start) | copy-done | bytes 524312
  8.3 0.0 copy-start.3
  8.4 0.1 collective-permute-start.5
  8.4 4.6 %collective-permute-start.2 = (bf16[512,128]{1,0:T(8,128)(2,1)S(1)}, bf16[512,128]{1,0:T(8,128)(2,1)S(1)}, u32[]{:S(2)}, u32[]{:S(2)}) collective-permute-start(bf16[512,128]{1,0:T(8,128)(2,1)S(1)} %pack.1.own_ref), channel_id=1, source_target_pairs={{0,16},{4,20},{8,24},{12,28},{1,17},{5,21},{9,25},{13,29},{2,18},{... | collective-permute-start | bytes 393224 | tf_op jit(solution)/shard_map/ppermute | solution.py:368
  13.1 1.6 %collective-permute-start.4 = (bf16[64,1024]{1,0:T(8,128)(2,1)S(1)}, bf16[64,1024]{1,0:T(8,128)(2,1)S(1)}, u32[]{:S(2)}, u32[]{:S(2)}) collective-permute-start(bf16[64,1024]{1,0:T(8,128)(2,1)S(1)} %get-tuple-element.35), channel_id=1, source_target_pairs={{0,2},{1,3},{2,0},{3,1},{4,6},{5,7},{6,4},{7,5},{8,10},{9,11},{10,... | collective-permute-start | bytes 393224 | tf_op jit(solution)/shard_map/ppermute | solution.py:372
  14.6 0.0 collective-permute-done.1.refs_0_
  14.6 0.0 collective-permute-done.5.refs_7_
  14.6 1.5 %collective-permute-start.6 = (bf16[512,128]{1,0:T(8,128)(2,1)S(1)}, bf16[512,128]{1,0:T(8,128)(2,1)S(1)}, u32[]{:S(2)}, u32[]{:S(2)}) collective-permute-start(bf16[512,128]{1,0:T(8,128)(2,1)S(1)} %collective-permute-done.1.refs_0_), channel_id=1, source_target_pairs={{0,4},{4,0},{8,12},{12,8},{16,20},{20,16},{24,28},{28,24},{1,5},{5... | collective-permute-start | bytes 393224 | tf_op jit(solution)/shard_map/ppermute | solution.py:372
  16.2 1.8 %collective-permute-start.3 = (bf16[512,128]{1,0:T(8,128)(2,1)S(1)}, bf16[512,128]{1,0:T(8,128)(2,1)S(1)}, u32[]{:S(2)}, u32[]{:S(2)}) collective-permute-start(bf16[512,128]{1,0:T(8,128)(2,1)S(1)} %pack.1.own_ref), channel_id=1, source_target_pairs={{0,24},{4,28},{1,25},{5,29},{2,26},{6,30},{3,27},{7,31}} | collective-permute-start | bytes 393224 | tf_op jit(solution)/shard_map/ppermute | solution.py:368
  17.9 0.0 copy-start.4
  17.9 0.1 collective-permute-start.7
  18.0 0.0 collective-permute-done.2.refs_1_
  18.0 0.6 collective-permute-done.4.refs_8_
  18.6 1.2 %collective-permute-done.6.refs_3_ = bf16[512,128]{1,0:T(8,128)(2,1)S(1)} collective-permute-done((bf16[512,128]{1,0:T(8,128)(2,1)S(1)}, bf16[512,128]{1,0:T(8,128)(2,1)S(1)}, u32[]{:S(2)}, u32[]{:S(2)}) %collective-permute-start.6) | collective-permute-done | bytes 131104 | tf_op jit(solution)/shard_map/ppermute | solution.py:372
  19.8 1.5 %collective-permute-start.8 = (bf16[512,128]{1,0:T(8,128)(2,1)S(1)}, bf16[512,128]{1,0:T(8,128)(2,1)S(1)}, u32[]{:S(2)}, u32[]{:S(2)}) collective-permute-start(bf16[512,128]{1,0:T(8,128)(2,1)S(1)} %collective-permute-done.2.refs_1_), channel_id=1, source_target_pairs={{0,4},{4,0},{8,12},{12,8},{16,20},{20,16},{24,28},{28,24},{1,5},{5... | collective-permute-start | bytes 393224 | tf_op jit(solution)/shard_map/ppermute | solution.py:372
  21.3 0.5 collective-permute-start
  21.9 0.0 collective-permute-done.3.refs_2_
  21.9 1.9 %collective-permute-done.7.refs_9_ = bf16[64,1024]{1,0:T(8,128)(2,1)S(1)} collective-permute-done((bf16[64,1024]{1,0:T(8,128)(2,1)S(1)}, bf16[64,1024]{1,0:T(8,128)(2,1)S(1)}, u32[]{:S(2)}, u32[]{:S(2)}) %collective-permute-start.7) | collective-permute-done | bytes 131104 | tf_op jit(solution)/shard_map/ppermute | solution.py:372
  23.8 2.4 %collective-permute-done.8.refs_4_ = bf16[512,128]{1,0:T(8,128)(2,1)S(1)} collective-permute-done((bf16[512,128]{1,0:T(8,128)(2,1)S(1)}, bf16[512,128]{1,0:T(8,128)(2,1)S(1)}, u32[]{:S(2)}, u32[]{:S(2)}) %collective-permute-start.8) | collective-permute-done | bytes 131104 | tf_op jit(solution)/shard_map/ppermute | solution.py:372
  26.2 0.9 %collective-permute-start.9 = (bf16[512,128]{1,0:T(8,128)(2,1)S(1)}, bf16[512,128]{1,0:T(8,128)(2,1)S(1)}, u32[]{:S(2)}, u32[]{:S(2)}) collective-permute-start(bf16[512,128]{1,0:T(8,128)(2,1)S(1)} %collective-permute-done.3.refs_2_), channel_id=1, source_target_pairs={{0,4},{4,0},{8,12},{12,8},{16,20},{20,16},{24,28},{28,24},{1,5},{5... | collective-permute-start | bytes 393224 | tf_op jit(solution)/shard_map/ppermute | solution.py:372
  27.1 1.9 %collective-permute-done.near_ref = bf16[512,128]{1,0:T(8,128)(2,1)S(1)} collective-permute-done((bf16[512,128]{1,0:T(8,128)(2,1)S(1)}, bf16[512,128]{1,0:T(8,128)(2,1)S(1)}, u32[]{:S(2)}, u32[]{:S(2)}) %collective-permute-start) | collective-permute-done | bytes 131104 | tf_op jit(solution)/shard_map/ppermute | solution.py:372
  29.0 2.2 %collective-permute-done.9.refs_5_ = bf16[512,128]{1,0:T(8,128)(2,1)S(1)} collective-permute-done((bf16[512,128]{1,0:T(8,128)(2,1)S(1)}, bf16[512,128]{1,0:T(8,128)(2,1)S(1)}, u32[]{:S(2)}, u32[]{:S(2)}) %collective-permute-start.9) | collective-permute-done | bytes 131104 | tf_op jit(solution)/shard_map/ppermute | solution.py:372
  31.2 0.0 copy-done.3
  31.2 0.0 copy-done.4
  31.2 8.3 %attention.1 = (bf16[64,1024]{1,0:T(8,128)(2,1)S(1)}, bf16[64,1024]{1,0:T(8,128)(2,1)S(1)}, bf16[64,1024]{1,0:T(8,128)(2,1)S(1)}, bf16[64,1024]{1,0:T(8,128)(2,1...) custom-call(s32[8]{0:T(128)S(1)} %copy-done.4, ...), custom_call_target="tpu_custom_call" | custom-call | flops 7516192768 | bytes 4194304 | tf_op jit(solution)/shard_map/attention/pallas_call | solution.py:214
  39.5 3.5 %collective-permute-start.14 = (bf16[2,256,256]{2,1,0:T(8,128)(2,1)S(1)}, bf16[2,256,256]{2,1,0:T(8,128)(2,1)S(1)}, u32[]{:S(2)}, u32[]{:S(2)}) collective-permute-start(bf16[2,256,256]{2,1,0:T(8,128)(2,1)S(1)} %get-tuple-element.57), channel_id=1, source_target_pairs={{0,4},{4,0},{8,12},{12,8},{16,20},{20,16},{24,28},{28,24},{1,5},{5... | collective-permute-start | bytes 786440 | tf_op jit(solution)/shard_map/ppermute | solution.py:372
  43.0 0.0 collective-permute-start.13
  43.0 7.2 %collective-permute-done.14.other_ref = bf16[2,256,256]{2,1,0:T(8,128)(2,1)S(1)} collective-permute-done((bf16[2,256,256]{2,1,0:T(8,128)(2,1)S(1)}, bf16[2,256,256]{2,1,0:T(8,128)(2,1)S(1)}, u32[]{:S(2)}, u32[]{:S(2)}) %collective-permute-start.14) | collective-permute-done | bytes 262176 | tf_op jit(solution)/shard_map/ppermute | solution.py:372
  50.2 0.1 merge.2
  50.3 1.3 %collective-permute-start.15 = (bf16[256,256]{1,0:T(8,128)(2,1)S(1)}, bf16[256,256]{1,0:T(8,128)(2,1)S(1)}, u32[]{:S(2)}, u32[]{:S(2)}) collective-permute-start(bf16[256,256]{1,0:T(8,128)(2,1)S(1)} %get-tuple-element.58), channel_id=1, source_target_pairs={{24,0},{28,4},{25,1},{29,5},{26,2},{30,6},{27,3},{31,7}} | collective-permute-start | bytes 393224 | tf_op jit(solution)/shard_map/ppermute | solution.py:368
  51.6 0.1 collective-permute-start.10
  51.7 0.6 collective-permute-start.11
  52.3 1.2 %collective-permute-start.12 = (bf16[64,1024]{1,0:T(8,128)(2,1)S(1)}, bf16[64,1024]{1,0:T(8,128)(2,1)S(1)}, u32[]{:S(2)}, u32[]{:S(2)}) collective-permute-start(bf16[64,1024]{1,0:T(8,128)(2,1)S(1)} %get-tuple-element.52), channel_id=1, source_target_pairs={{0,3},{1,2},{2,1},{3,0},{4,7},{5,6},{6,5},{7,4},{8,11},{9,10},{10,... | collective-permute-start | bytes 393224 | tf_op jit(solution)/shard_map/ppermute | solution.py:372
  53.5 0.0 collective-permute-done.13.other_ref
  53.5 1.3 %collective-permute-start.16 = (bf16[256,256]{1,0:T(8,128)(2,1)S(1)}, bf16[256,256]{1,0:T(8,128)(2,1)S(1)}, u32[]{:S(2)}, u32[]{:S(2)}) collective-permute-start(bf16[256,256]{1,0:T(8,128)(2,1)S(1)} %get-tuple-element.62), channel_id=1, source_target_pairs={{16,0},{20,4},{24,8},{28,12},{17,1},{21,5},{25,9},{29,13},{18,2},{... | collective-permute-start | bytes 393224 | tf_op jit(solution)/shard_map/ppermute | solution.py:368
  54.8 18.8 %collective-permute-done.15.refs_0_ = bf16[256,256]{1,0:T(8,128)(2,1)S(1)} collective-permute-done((bf16[256,256]{1,0:T(8,128)(2,1)S(1)}, bf16[256,256]{1,0:T(8,128)(2,1)S(1)}, u32[]{:S(2)}, u32[]{:S(2)}) %collective-permute-start.15) | collective-permute-done | bytes 131104 | tf_op jit(solution)/shard_map/ppermute | solution.py:368
  73.6 0.1 merge.3
  73.7 1.3 %collective-permute-start.17 = (bf16[256,256]{1,0:T(8,128)(2,1)S(1)}, bf16[256,256]{1,0:T(8,128)(2,1)S(1)}, u32[]{:S(2)}, u32[]{:S(2)}) collective-permute-start(bf16[256,256]{1,0:T(8,128)(2,1)S(1)} %get-tuple-element.63), channel_id=1, source_target_pairs={{8,0},{12,4},{16,8},{20,12},{24,16},{28,20},{9,1},{13,5},{17,9},{2... | collective-permute-start | bytes 393224 | tf_op jit(solution)/shard_map/ppermute | solution.py:368
  75.0 0.0 collective-permute-done.10.refs_1_
  75.0 0.0 collective-permute-done.11.refs_2_
  75.0 0.0 collective-permute-done.12.refs_3_
  75.0 0.8 %join.1 = bf16[64,4096]{1,0:T(8,128)(2,1)} custom-call(bf16[64,1024]{1,0:T(8,128)(2,1)S(1)} %get-tuple-element.49.refs_0_, bf16[64,1024]{1,0:T(8,128)(2,1)S(1)} %collective-permute-done.10.refs_1_, bf16[64,1024]{1,0:T(8,128)(2,1)S(1)} %collective-permute-done.11.refs_2_, bf16[64,1024]{1,0:T(8,128)(2,1)S(1)} %collective-permute-done.12.refs_3_), custom_call_target="tpu_custom_call" | custom-call | tf_op jit(solution)/shard_map/join/pallas_call | solution.py:312
  75.9 0.0 collective-permute-done.16.refs_1_
  75.9 4.7 %collective-permute-done.17.refs_2_ = bf16[256,256]{1,0:T(8,128)(2,1)S(1)} collective-permute-done((bf16[256,256]{1,0:T(8,128)(2,1)S(1)}, bf16[256,256]{1,0:T(8,128)(2,1)S(1)}, u32[]{:S(2)}, u32[]{:S(2)}) %collective-permute-start.17) | collective-permute-done | bytes 131104 | tf_op jit(solution)/shard_map/ppermute | solution.py:368
  80.5 0.9 %finish.1 = (bf16[256,128]{1,0:T(8,128)(2,1)}, bf16[256,128]{1,0:T(8,128)(2,1)}) custom-call(f32[256,256]{1,0:T(8,128)S(1)} %get-tuple-element.60.own_ref, bf16[256,256]{1,0:T(8,128)(2,1)S(1)} %collective-permute-done.15.refs_0_, bf16[256,256]{1,0:T(8,128)(2,1)S(1)} %collective-permute-done.16.refs_1_, bf16[256,256]{1,0:T(8,128)(2,1)S(1)} %collective-permute-done.17.refs_2_), custom_call_target="tpu_custom_call" | custom-call | tf_op jit(solution)/shard_map/finish/pallas_call | solution.py:356
  (2 shorter events, 0.0 us)
Async XLA Ops:
  0.6 0.8 %copy-start.1 = (bf16[256,1,128]{2,0,1:T(8,128)(2,1)S(1)}, bf16[256,1,128]{2,0,1:T(8,128)(2,1)}, u32[]{:S(2)}) copy-start(bf16[256,1,128]{2,0,1:T(8,128)(2,1)} %param.6) | copy-start | bytes 196612
  1.5 0.8 %copy-start.2 = (bf16[256,1,128]{2,0,1:T(8,128)(2,1)S(1)}, bf16[256,1,128]{2,0,1:T(8,128)(2,1)}, u32[]{:S(2)}) copy-start(bf16[256,1,128]{2,0,1:T(8,128)(2,1)} %param.7) | copy-start | bytes 196612
  2.3 12.3 %collective-permute-start.1 = (bf16[512,128]{1,0:T(8,128)(2,1)S(1)}, bf16[512,128]{1,0:T(8,128)(2,1)S(1)}, u32[]{:S(2)}, u32[]{:S(2)}) collective-permute-start(bf16[512,128]{1,0:T(8,128)(2,1)S(1)} %pack.1.own_ref), channel_id=1, source_target_pairs={{0,8},{4,12},{8,16},{12,20},{16,24},{20,28},{1,9},{5,13},{9,17},{1... | collective-permute-start | bytes 393224 | tf_op jit(solution)/shard_map/ppermute | solution.py:368
  7.3 1.0 %copy-start = (bf16[64,4096]{1,0:T(8,128)(2,1)S(1)}, bf16[64,4096]{1,0:T(8,128)(2,1)}, u32[]{:S(2)}) copy-start(bf16[64,4096]{1,0:T(8,128)(2,1)} %grad_ref.1) | copy-start | bytes 1572868
  8.3 22.9 %copy-start.3 = (bf16[256,8,128]{2,1,0:T(8,128)(2,1)S(1)}, bf16[256,8,128]{2,1,0:T(8,128)(2,1)}, u32[]{:S(2)}) copy-start(bf16[256,8,128]{2,1,0:T(8,128)(2,1)} %q_ref.1) | copy-start | bytes 1572868
  8.4 6.3 %collective-permute-start.5 = (bf16[64,1024]{1,0:T(8,128)(2,1)S(1)}, bf16[64,1024]{1,0:T(8,128)(2,1)S(1)}, u32[]{:S(2)}, u32[]{:S(2)}) collective-permute-start(bf16[64,1024]{1,0:T(8,128)(2,1)S(1)} %get-tuple-element.37), channel_id=1, source_target_pairs={{0,1},{1,0},{2,3},{3,2},{4,5},{5,4},{6,7},{7,6},{8,9},{9,8},{10,11... | collective-permute-start | bytes 393224 | tf_op jit(solution)/shard_map/ppermute | solution.py:372
  8.4 9.6 %collective-permute-start.2 = (bf16[512,128]{1,0:T(8,128)(2,1)S(1)}, bf16[512,128]{1,0:T(8,128)(2,1)S(1)}, u32[]{:S(2)}, u32[]{:S(2)}) collective-permute-start(bf16[512,128]{1,0:T(8,128)(2,1)S(1)} %pack.1.own_ref), channel_id=1, source_target_pairs={{0,16},{4,20},{8,24},{12,28},{1,17},{5,21},{9,25},{13,29},{2,18},{... | collective-permute-start | bytes 393224 | tf_op jit(solution)/shard_map/ppermute | solution.py:368
  13.1 5.5 %collective-permute-start.4 = (bf16[64,1024]{1,0:T(8,128)(2,1)S(1)}, bf16[64,1024]{1,0:T(8,128)(2,1)S(1)}, u32[]{:S(2)}, u32[]{:S(2)}) collective-permute-start(bf16[64,1024]{1,0:T(8,128)(2,1)S(1)} %get-tuple-element.35), channel_id=1, source_target_pairs={{0,2},{1,3},{2,0},{3,1},{4,6},{5,7},{6,4},{7,5},{8,10},{9,11},{10,... | collective-permute-start | bytes 393224 | tf_op jit(solution)/shard_map/ppermute | solution.py:372
  14.6 5.2 %collective-permute-start.6 = (bf16[512,128]{1,0:T(8,128)(2,1)S(1)}, bf16[512,128]{1,0:T(8,128)(2,1)S(1)}, u32[]{:S(2)}, u32[]{:S(2)}) collective-permute-start(bf16[512,128]{1,0:T(8,128)(2,1)S(1)} %collective-permute-done.1.refs_0_), channel_id=1, source_target_pairs={{0,4},{4,0},{8,12},{12,8},{16,20},{20,16},{24,28},{28,24},{1,5},{5... | collective-permute-start | bytes 393224 | tf_op jit(solution)/shard_map/ppermute | solution.py:372
  16.2 5.7 %collective-permute-start.3 = (bf16[512,128]{1,0:T(8,128)(2,1)S(1)}, bf16[512,128]{1,0:T(8,128)(2,1)S(1)}, u32[]{:S(2)}, u32[]{:S(2)}) collective-permute-start(bf16[512,128]{1,0:T(8,128)(2,1)S(1)} %pack.1.own_ref), channel_id=1, source_target_pairs={{0,24},{4,28},{1,25},{5,29},{2,26},{6,30},{3,27},{7,31}} | collective-permute-start | bytes 393224 | tf_op jit(solution)/shard_map/ppermute | solution.py:368
  17.9 13.2 %copy-start.4 = (s32[8]{0:T(128)S(1)}, s32[8]{0:T(128)}, u32[]{:S(2)}) copy-start(s32[8]{0:T(128)} %doc_ref.1) | copy-start | bytes 100
  17.9 5.8 %collective-permute-start.7 = (bf16[64,1024]{1,0:T(8,128)(2,1)S(1)}, bf16[64,1024]{1,0:T(8,128)(2,1)S(1)}, u32[]{:S(2)}, u32[]{:S(2)}) collective-permute-start(bf16[64,1024]{1,0:T(8,128)(2,1)S(1)} %get-tuple-element.40), channel_id=1, source_target_pairs={{0,3},{1,2},{2,1},{3,0},{4,7},{5,6},{6,5},{7,4},{8,11},{9,10},{10,... | collective-permute-start | bytes 393224 | tf_op jit(solution)/shard_map/ppermute | solution.py:372
  19.8 6.4 %collective-permute-start.8 = (bf16[512,128]{1,0:T(8,128)(2,1)S(1)}, bf16[512,128]{1,0:T(8,128)(2,1)S(1)}, u32[]{:S(2)}, u32[]{:S(2)}) collective-permute-start(bf16[512,128]{1,0:T(8,128)(2,1)S(1)} %collective-permute-done.2.refs_1_), channel_id=1, source_target_pairs={{0,4},{4,0},{8,12},{12,8},{16,20},{20,16},{24,28},{28,24},{1,5},{5... | collective-permute-start | bytes 393224 | tf_op jit(solution)/shard_map/ppermute | solution.py:372
  21.3 7.7 %collective-permute-start = (bf16[512,128]{1,0:T(8,128)(2,1)S(1)}, bf16[512,128]{1,0:T(8,128)(2,1)S(1)}, u32[]{:S(2)}, u32[]{:S(2)}) collective-permute-start(bf16[512,128]{1,0:T(8,128)(2,1)S(1)} %pack.1.own_ref), channel_id=1, source_target_pairs={{0,4},{4,0},{8,12},{12,8},{16,20},{20,16},{24,28},{28,24},{1,5},{5... | collective-permute-start | bytes 393224 | tf_op jit(solution)/shard_map/ppermute | solution.py:372
  26.2 5.0 %collective-permute-start.9 = (bf16[512,128]{1,0:T(8,128)(2,1)S(1)}, bf16[512,128]{1,0:T(8,128)(2,1)S(1)}, u32[]{:S(2)}, u32[]{:S(2)}) collective-permute-start(bf16[512,128]{1,0:T(8,128)(2,1)S(1)} %collective-permute-done.3.refs_2_), channel_id=1, source_target_pairs={{0,4},{4,0},{8,12},{12,8},{16,20},{20,16},{24,28},{28,24},{1,5},{5... | collective-permute-start | bytes 393224 | tf_op jit(solution)/shard_map/ppermute | solution.py:372
  39.5 10.7 %collective-permute-start.14 = (bf16[2,256,256]{2,1,0:T(8,128)(2,1)S(1)}, bf16[2,256,256]{2,1,0:T(8,128)(2,1)S(1)}, u32[]{:S(2)}, u32[]{:S(2)}) collective-permute-start(bf16[2,256,256]{2,1,0:T(8,128)(2,1)S(1)} %get-tuple-element.57), channel_id=1, source_target_pairs={{0,4},{4,0},{8,12},{12,8},{16,20},{20,16},{24,28},{28,24},{1,5},{5... | collective-permute-start | bytes 786440 | tf_op jit(solution)/shard_map/ppermute | solution.py:372
  43.0 10.5 %collective-permute-start.13 = (bf16[2,256,256]{2,1,0:T(8,128)(2,1)S(1)}, bf16[2,256,256]{2,1,0:T(8,128)(2,1)S(1)}, u32[]{:S(2)}, u32[]{:S(2)}) collective-permute-start(bf16[2,256,256]{2,1,0:T(8,128)(2,1)S(1)} %get-tuple-element.55), channel_id=1, source_target_pairs={{0,4},{4,0},{8,12},{12,8},{16,20},{20,16},{24,28},{28,24},{1,5},{5... | collective-permute-start | bytes 786440 | tf_op jit(solution)/shard_map/ppermute | solution.py:372
  50.3 23.3 %collective-permute-start.15 = (bf16[256,256]{1,0:T(8,128)(2,1)S(1)}, bf16[256,256]{1,0:T(8,128)(2,1)S(1)}, u32[]{:S(2)}, u32[]{:S(2)}) collective-permute-start(bf16[256,256]{1,0:T(8,128)(2,1)S(1)} %get-tuple-element.58), channel_id=1, source_target_pairs={{24,0},{28,4},{25,1},{29,5},{26,2},{30,6},{27,3},{31,7}} | collective-permute-start | bytes 393224 | tf_op jit(solution)/shard_map/ppermute | solution.py:368
  51.6 23.4 %collective-permute-start.10 = (bf16[64,1024]{1,0:T(8,128)(2,1)S(1)}, bf16[64,1024]{1,0:T(8,128)(2,1)S(1)}, u32[]{:S(2)}, u32[]{:S(2)}) collective-permute-start(bf16[64,1024]{1,0:T(8,128)(2,1)S(1)} %get-tuple-element.50), channel_id=1, source_target_pairs={{0,1},{1,0},{2,3},{3,2},{4,5},{5,4},{6,7},{7,6},{8,9},{9,8},{10,11... | collective-permute-start | bytes 393224 | tf_op jit(solution)/shard_map/ppermute | solution.py:372
  51.7 23.3 %collective-permute-start.11 = (bf16[64,1024]{1,0:T(8,128)(2,1)S(1)}, bf16[64,1024]{1,0:T(8,128)(2,1)S(1)}, u32[]{:S(2)}, u32[]{:S(2)}) collective-permute-start(bf16[64,1024]{1,0:T(8,128)(2,1)S(1)} %get-tuple-element.51), channel_id=1, source_target_pairs={{0,2},{1,3},{2,0},{3,1},{4,6},{5,7},{6,4},{7,5},{8,10},{9,11},{10,... | collective-permute-start | bytes 393224 | tf_op jit(solution)/shard_map/ppermute | solution.py:372
  52.3 22.7 %collective-permute-start.12 = (bf16[64,1024]{1,0:T(8,128)(2,1)S(1)}, bf16[64,1024]{1,0:T(8,128)(2,1)S(1)}, u32[]{:S(2)}, u32[]{:S(2)}) collective-permute-start(bf16[64,1024]{1,0:T(8,128)(2,1)S(1)} %get-tuple-element.52), channel_id=1, source_target_pairs={{0,3},{1,2},{2,1},{3,0},{4,7},{5,6},{6,5},{7,4},{8,11},{9,10},{10,... | collective-permute-start | bytes 393224 | tf_op jit(solution)/shard_map/ppermute | solution.py:372
  53.5 22.3 %collective-permute-start.16 = (bf16[256,256]{1,0:T(8,128)(2,1)S(1)}, bf16[256,256]{1,0:T(8,128)(2,1)S(1)}, u32[]{:S(2)}, u32[]{:S(2)}) collective-permute-start(bf16[256,256]{1,0:T(8,128)(2,1)S(1)} %get-tuple-element.62), channel_id=1, source_target_pairs={{16,0},{20,4},{24,8},{28,12},{17,1},{21,5},{25,9},{29,13},{18,2},{... | collective-permute-start | bytes 393224 | tf_op jit(solution)/shard_map/ppermute | solution.py:368
  73.7 6.9 %collective-permute-start.17 = (bf16[256,256]{1,0:T(8,128)(2,1)S(1)}, bf16[256,256]{1,0:T(8,128)(2,1)S(1)}, u32[]{:S(2)}, u32[]{:S(2)}) collective-permute-start(bf16[256,256]{1,0:T(8,128)(2,1)S(1)} %get-tuple-element.63), channel_id=1, source_target_pairs={{8,0},{12,4},{16,8},{20,12},{24,16},{28,20},{9,1},{13,5},{17,9},{2... | collective-permute-start | bytes 393224 | tf_op jit(solution)/shard_map/ppermute | solution.py:368
